TPU v7x, 32 devices: a whole 2x2x4 slice. The times are simulated.
32 devices in a mesh: dp: 16 (over z, x, core), rep: 2 (over y).
Axes of the slice: x: 2, y: 2, z: 4, core: 2. Of those that a mesh axis runs over, the one named last changes fastest.
Arguments:
- hidden_in: bfloat16 [128, 512, 576], P(('dp', 'rep')), may hold values from -6 to 6
- segment_ids: int32 [128, 512], P(('dp', 'rep')), may hold values from 0 to 5, never falling along the last dimension, each value on 1 to 256 neighbouring positions
- gain_attn: bfloat16 [576], replicated, may hold values from 0.099609375 to 1.8984375
- w_query: bfloat16 [331776], P('dp'), may hold values from -0.25 to 0.25
- w_key: bfloat16 [110592], P('dp'), may hold values from -0.25 to 0.25
- w_value: bfloat16 [110592], P('dp'), may hold values from -0.25 to 0.25
- w_out: bfloat16 [331776], P('dp'), may hold values from -1 to 1
- gain_mlp: bfloat16 [576], replicated, may hold values from 0.099609375 to 1.8984375
- w_gate: bfloat16 [884736], P('dp'), may hold values from -0.25 to 0.25
- w_up: bfloat16 [884736], P('dp'), may hold values from -0.25 to 0.25
- w_down: bfloat16 [884736], P('dp'), may hold values from -0.21875 to 0.21875
- cotangent: bfloat16 [128, 512, 576], P(('dp', 'rep')), may hold values from -6 to 6
Outputs:
- hidden_out: bfloat16 [128, 512, 576], P(('dp', 'rep'))
- grad_hidden: bfloat16 [128, 512, 576], P(('dp', 'rep'))
- grad_gain_attn: float32 [576], replicated
- grad_query: float32 [331776], P('dp')
- grad_key: float32 [110592], P('dp')
- grad_value: float32 [110592], P('dp')
- grad_out: float32 [331776], P('dp')
- grad_gain_mlp: float32 [576], replicated
- grad_gate: float32 [884736], P('dp')
- grad_up: float32 [884736], P('dp')
- grad_down: float32 [884736], P('dp')
Inputs may be any that keep to these rules, and one draw needn't show every extreme that they name: `segment_ids`: within each sequence the numbers never fall; one document holds at most half of 512 tokens.
All inputs are finite; a program needn't handle non-finite values.
Results may differ from a plain program's by a relative error of at most 0.014.
Values may be sent and summed in bfloat16 or wider, within the bound.
A program may use at most 192 MiB of HBM per device.

v0:
```python
import functools

import jax
import jax.numpy as jnp
from jax import lax
from jax.experimental import pallas as pl
from jax.experimental.pallas import tpu as pltpu
from jax.sharding import PartitionSpec as P

D = 576
HEADS = 9
KV_HEADS = 3
GROUP = HEADS // KV_HEADS
HEAD_DIM = 64
HALF = HEAD_DIM // 2
KV_W = KV_HEADS * HEAD_DIM
QKV = D + 2 * KV_W
FF = 1536
SEQ = 512
QB = 256

EPS = 1e-05
THETA = 100000.0
SCALE = HEAD_DIM ** (-0.5)
F32 = jnp.float32
BF16 = jnp.bfloat16

BLOCKS = ((0, QB, 0), (QB, SEQ, QB))
ROWS = QB + SEQ


def dot(a, b, ca, cb):
    return lax.dot_general(a, b, (((ca,), (cb,)), ((), ())), preferred_element_type=F32)


def turn_t(u):
    return jnp.concatenate([-u[HALF:], u[:HALF]], axis=0)


def attend_kernel(qkv_ref, cos_ref, sin_ref, start_ref, *refs):
    p_ref, o_ref, q_ref, k_ref, v_ref, bias_ref = refs[-6:]
    cos, sin = cos_ref[...], sin_ref[...]
    start = start_ref[0]
    key_at = lax.broadcasted_iota(jnp.int32, (SEQ, SEQ), 0)
    query_at = lax.broadcasted_iota(jnp.int32, (SEQ, SEQ), 1)
    ok = jnp.logical_and(key_at <= query_at, key_at >= start)
    bias_ref[...] = jnp.where(ok, 0.0, -1e30)
    v_ref[...] = qkv_ref[D + KV_W :, :].astype(BF16)
    for g in range(KV_HEADS):
        raw = qkv_ref[D + g * HEAD_DIM : D + (g + 1) * HEAD_DIM, :]
        kt = raw * cos + turn_t(raw) * sin
        k_ref[g * HEAD_DIM : (g + 1) * HEAD_DIM, :] = kt.astype(BF16)
        k = kt.T.astype(BF16)
        vt = v_ref[g * HEAD_DIM : (g + 1) * HEAD_DIM, :]
        for j in range(GROUP):
            h = g * GROUP + j
            rows = slice(h * HEAD_DIM, (h + 1) * HEAD_DIM)
            raw = qkv_ref[rows, :]
            qt = (raw * cos + turn_t(raw) * sin).astype(BF16) * jnp.asarray(SCALE, BF16)
            q_ref[rows, :] = qt
            for q0, nk, r0 in BLOCKS:
                st = dot(k[:nk], qt[:, q0 : q0 + QB], 1, 0) + bias_ref[:nk, q0 : q0 + QB]
                top = jnp.max(st, axis=0, keepdims=True)
                e = jnp.exp(st - top)
                total = jnp.sum(e, axis=0, keepdims=True)
                share = (e * (1.0 / total)).astype(BF16)
                p_ref[0, h, r0 : r0 + nk, :] = share
                o_ref[rows, q0 : q0 + QB] = dot(vt[:, :nk], share, 1, 0).astype(BF16)


def attend_forward(qkv, cos, sin, start, first, seqs, after, o_before):
    tokens = qkv.shape[1]
    col = lambda rows: pl.BlockSpec((rows, SEQ), lambda s: (0, s + first))
    own = lambda rows: pl.BlockSpec((rows, SEQ), lambda s: (0, s))
    extra = [*after] + ([] if o_before is None else [o_before])
    return pl.pallas_call(
        attend_kernel,
        grid=(seqs,),
        in_specs=[
            col(QKV),
            col(HEAD_DIM),
            col(HEAD_DIM),
            pl.BlockSpec((1, 1, SEQ), lambda s: (s + first, 0, 0)),
            *[pl.BlockSpec(memory_space=pl.ANY) for _ in extra],
        ],
        out_specs=[
            pl.BlockSpec((1, HEADS, ROWS, QB), lambda s: (s, 0, 0, 0)),
            col(D),
            own(D),
            own(KV_W),
            own(KV_W),
        ],
        out_shape=[
            jax.ShapeDtypeStruct((seqs, HEADS, ROWS, QB), BF16),
            jax.ShapeDtypeStruct((D, tokens), BF16),
            jax.ShapeDtypeStruct((D, seqs * SEQ), BF16),
            jax.ShapeDtypeStruct((KV_W, seqs * SEQ), BF16),
            jax.ShapeDtypeStruct((KV_W, seqs * SEQ), BF16),
        ],
        input_output_aliases={} if o_before is None else {3 + len(extra): 1},
        scratch_shapes=[pltpu.VMEM((SEQ, SEQ), F32)],
        compiler_params=pltpu.CompilerParams(vmem_limit_bytes=40 * 2**20),
        cost_estimate=pl.CostEstimate(
            flops=seqs * 5_000_000_000, bytes_accessed=seqs * 8_000_000, transcendentals=seqs * 1_800_000
        ),
        name="attend_forward",
    )(qkv, cos, sin, start, *extra)


def attend_back_kernel(p_ref, o_ref, do_ref, q_ref, k_ref, v_ref, cos_ref, sin_ref, *refs):
    d_ref = refs[-1]
    cos, sin = cos_ref[...], sin_ref[...]

    def unturn(u):
        return (u * cos - turn_t(u) * sin).astype(BF16)

    for g in range(KV_HEADS):
        kt = k_ref[g * HEAD_DIM : (g + 1) * HEAD_DIM, :]
        v = v_ref[g * HEAD_DIM : (g + 1) * HEAD_DIM, :].T
        dk = [None, None]
        dv = [None, None]
        for j in range(GROUP):
            h = g * GROUP + j
            rows = slice(h * HEAD_DIM, (h + 1) * HEAD_DIM)
            dot_t = do_ref[rows, :]
            inner = jnp.sum(dot_t.astype(F32) * o_ref[rows, :].astype(F32), axis=0, keepdims=True)
            q = q_ref[rows, :].T
            do = dot_t.T
            dq = []
            for b, (q0, nk, r0) in enumerate(BLOCKS):
                share = p_ref[0, h, r0 : r0 + nk, :]
                dp = dot(v[:nk], dot_t[:, q0 : q0 + QB], 1, 0)
                ds = (share.astype(F32) * (dp - inner[:, q0 : q0 + QB])).astype(BF16)
                dq.append(dot(kt[:, :nk], ds, 1, 0))
                dk_new = dot(ds, q[q0 : q0 + QB], 1, 0)
                dv_new = dot(share, do[q0 : q0 + QB], 1, 0)
                dk[b] = dk_new if dk[b] is None else dk[b] + dk_new
                dv[b] = dv_new if dv[b] is None else dv[b] + dv_new
            d_ref[rows, :] = unturn(jnp.concatenate(dq, axis=1) * SCALE)
        dk_all = jnp.concatenate([dk[0] + dk[1][:QB], dk[1][QB:]], axis=0)
        dv_all = jnp.concatenate([dv[0] + dv[1][:QB], dv[1][QB:]], axis=0)
        d_ref[D + g * HEAD_DIM : D + (g + 1) * HEAD_DIM, :] = unturn(dk_all.T)
        d_ref[D + KV_W + g * HEAD_DIM : D + KV_W + (g + 1) * HEAD_DIM, :] = dv_all.T.astype(BF16)


def attend_backward(share, o, do, q, k, v, cos, sin, first, after, d_before):
    tokens = o.shape[1]
    seqs = share.shape[0]
    col = lambda rows: pl.BlockSpec((rows, SEQ), lambda s: (0, s + first))
    own = lambda rows: pl.BlockSpec((rows, SEQ), lambda s: (0, s))
    extra = [*after] + ([] if d_before is None else [d_before])
    return pl.pallas_call(
        attend_back_kernel,
        grid=(seqs,),
        in_specs=[
            pl.BlockSpec((1, HEADS, ROWS, QB), lambda s: (s, 0, 0, 0)),
            col(D),
            col(D),
            own(D),
            own(KV_W),
            own(KV_W),
            col(HEAD_DIM),
            col(HEAD_DIM),
            *[pl.BlockSpec(memory_space=pl.ANY) for _ in extra],
        ],
        out_specs=col(QKV),
        out_shape=jax.ShapeDtypeStruct((QKV, tokens), BF16),
        input_output_aliases={} if d_before is None else {7 + len(extra): 0},
        compiler_params=pltpu.CompilerParams(vmem_limit_bytes=40 * 2**20),
        cost_estimate=pl.CostEstimate(
            flops=seqs * 10_000_000_000, bytes_accessed=seqs * 8_000_000, transcendentals=0
        ),
        name="attend_backward",
    )(share, o, do, q, k, v, cos, sin, *extra)


def swap(x, axis, size, bit):
    return lax.ppermute(x, axis, [(i, i ^ bit) for i in range(size)])


def bits_of(size):
    return [1 << n for n in range(size.bit_length() - 1)]


def upper(bit):
    return (lax.axis_index("dp") & bit) != 0


def gather_far(block, size):
    far = size // 4
    held = [block] + [swap(block, "dp", size, 4 * n) for n in range(1, far)]
    for bit in bits_of(far):
        up = upper(4 * bit)
        held = [jnp.where(up, held[n ^ bit], held[n]) for n in range(far)]
    return jnp.stack(held)


def gather_pair(held, size, bit):
    other = swap(held, "dp", size, bit)
    up = upper(bit)
    return jnp.stack([jnp.where(up, other, held), jnp.where(up, held, other)])


def gather_end(held):
    return held.transpose(2, 1, 0, 3, 4).reshape(-1, held.shape[-1])


def scatter_begin(whole, size):
    rows = whole.shape[0] // size
    return whole.astype(BF16).reshape(size // 4, 2, 2, rows, whole.shape[1])


def scatter_pair(held, size, bit, axis):
    side = upper(bit).astype(jnp.int32)
    keep = lax.dynamic_index_in_dim(held, side, axis, keepdims=False)
    send = lax.dynamic_index_in_dim(held, 1 - side, axis, keepdims=False)
    got = swap(send, "dp", size, bit)
    return (keep.astype(F32) + got.astype(F32)).astype(BF16)


def scatter_far(held, size):
    mine = lax.axis_index("dp") // 4
    block = lambda n: lax.dynamic_index_in_dim(held, mine ^ n, 0, keepdims=False)
    total = block(0).astype(F32)
    for n in range(1, size // 4):
        total = total + swap(block(n), "dp", size, 4 * n).astype(F32)
    return total.astype(BF16)


def scatter_rep(held, rep):
    return held.astype(F32) + swap(held, "rep", rep, 1).astype(F32)


def token(held):
    return held.reshape((-1,) + held.shape[-2:])[0, :16, :128]


def sum_small(x, size, rep):
    for bit in bits_of(size):
        x = x + swap(x, "dp", size, bit)
    return x + swap(x, "rep", rep, 1)


def per_device(
    size,
    rep,
    hidden_in,
    segment_ids,
    gain_attn,
    w_query,
    w_key,
    w_value,
    w_out,
    gain_mlp,
    w_gate,
    w_up,
    w_down,
    cotangent,
):
    by_rows = size >= 4 and D % size == 0 and FF % size == 0 and size & (size - 1) == 0 and rep == 2
    if by_rows:
        part = D // size
        mats = [
            w.reshape(part, -1) for w in (w_query, w_key, w_value, w_out, w_gate, w_up)
        ]
        attn_far = gather_far(jnp.concatenate(mats[:4], axis=1), size)
        mlp_block, attn_far = lax.optimization_barrier(
            (jnp.concatenate(mats[4:], axis=1), attn_far)
        )
        mlp_far = gather_far(mlp_block, size)
        attn_w = gather_end(gather_pair(gather_pair(attn_far, size, 2), size, 1))
        down_block, mlp_far = lax.optimization_barrier((w_down.reshape(FF // size, D), mlp_far))
        mlp_x = gather_pair(mlp_far, size, 2)
        down_far = gather_far(down_block, size)
        mlp_w = gather_end(gather_pair(mlp_x, size, 1))
        down_w = gather_end(gather_pair(gather_pair(down_far, size, 2), size, 1))
        after_first, after_second = (token(mlp_far),), (token(mlp_x), token(down_far))
    else:
        whole = [
            lax.all_gather(w, "dp", axis=0, tiled=True).reshape(D, -1)
            for w in (w_query, w_key, w_value, w_out, w_gate, w_up)
        ]
        attn_w = jnp.concatenate(whole[:4], axis=1)
        mlp_w = jnp.concatenate(whole[4:], axis=1)
        down_w = lax.all_gather(w_down, "dp", axis=0, tiled=True).reshape(FF, D)
        after_first, after_second = (), ()
    qkv_w, out_w = attn_w[:, :QKV], attn_w[:, QKV:]
    gate_w, up_w = mlp_w[:, :FF], mlp_w[:, FF:]

    seqs = hidden_in.shape[0]
    tokens = seqs * SEQ
    gain_first = gain_attn.astype(F32)
    gain_second = gain_mlp.astype(F32)

    start = jnp.sum(
        (segment_ids[:, None, :] < segment_ids[:, :, None]).astype(jnp.int32), axis=-1
    )
    place = (jnp.arange(SEQ, dtype=jnp.int32)[None, :] - start).astype(F32).reshape(1, tokens)
    inverse = THETA ** (-(jnp.arange(HALF, dtype=F32) * (2.0 / HEAD_DIM)))
    angle = inverse[:, None] * place
    cos, sin = jnp.cos(angle), jnp.sin(angle)
    cos = jnp.concatenate([cos, cos], axis=0)
    sin = jnp.concatenate([sin, sin], axis=0)

    x = hidden_in.reshape(tokens, D).astype(F32)
    r1 = lax.rsqrt(jnp.mean(x * x, axis=-1, keepdims=True) + EPS)
    h1 = (x * r1 * gain_first).astype(BF16)
    qkv = dot(qkv_w, h1, 0, 1)
    start = start.reshape(seqs, 1, SEQ)
    half = seqs // 2
    share0, o, q0, k0, v0 = attend_forward(qkv, cos, sin, start, 0, half, after_first, None)
    share1, o, q1, k1, v1 = attend_forward(
        qkv, cos, sin, start, half, seqs - half, after_second, o
    )
    m = x + dot(o, out_w, 0, 0)
    r2 = lax.rsqrt(jnp.mean(m * m, axis=-1, keepdims=True) + EPS)
    h2 = (m * r2 * gain_second).astype(BF16)
    a = dot(h2, gate_w, 1, 0)
    b = dot(h2, up_w, 1, 0)
    s = jax.nn.sigmoid(a)
    c = (a * s * b).astype(BF16)
    result = (m + dot(c, down_w, 1, 0)).astype(BF16)

    gy = cotangent.reshape(tokens, D)
    d_down = dot(c, gy, 0, 0)
    if by_rows:
        d_down, gy = lax.optimization_barrier((d_down.astype(BF16), gy))
        down_core = scatter_pair(scatter_begin(d_down, size), size, 1, 2)
    dc = dot(gy, down_w, 1, 1)
    da = (dc * b * s * (1.0 + a * (1.0 - s))).astype(BF16)
    db = (dc * a * s).astype(BF16)
    d_gate = dot(h2, da, 0, 0)
    d_up = dot(h2, db, 0, 0)
    after_first, after_second = (), ()
    if by_rows:
        d_gu = jnp.concatenate([d_gate.astype(BF16), d_up.astype(BF16)], axis=1)
        d_gu, down_core, da, db = lax.optimization_barrier((d_gu, down_core, da, db))
        gu_core = scatter_pair(scatter_begin(d_gu, size), size, 1, 2)
        down_x = scatter_pair(down_core, size, 2, 1)
    dh2 = dot(da, gate_w, 1, 1) + dot(db, up_w, 1, 1)
    g2 = jnp.sum(dh2 * m * r2, axis=0)
    e = dh2 * gain_second
    dm = gy.astype(F32) + r2 * (e - m * r2 * r2 * jnp.mean(e * m, axis=-1, keepdims=True))
    dmb = dm.astype(BF16)
    d_out = dot(o, dmb, 1, 0)
    do = dot(out_w, dmb, 1, 1).astype(BF16)
    if by_rows:
        gu_x = scatter_pair(gu_core, size, 2, 1)
        down_z = scatter_far(down_x, size)
        out_core = scatter_pair(scatter_begin(d_out, size), size, 1, 2)
        after_first = (token(gu_core), token(down_x))
        after_second = (token(gu_x), token(out_core), token(down_z))
    dqkv = attend_backward(share0, o, do, q0, k0, v0, cos, sin, 0, after_first, None)
    dqkv = attend_backward(share1, o, do, q1, k1, v1, cos, sin, half, after_second, dqkv)
    d_qkv = dot(h1, dqkv, 0, 1)
    dh1 = dot(dqkv, qkv_w, 0, 1)
    g1 = jnp.sum(dh1 * x * r1, axis=0)
    e1 = dh1 * gain_first
    dx = dm + r1 * (e1 - x * r1 * r1 * jnp.mean(e1 * x, axis=-1, keepdims=True))
    grad_hidden = dx.astype(BF16)

    if by_rows:
        d_down = scatter_rep(down_z, rep)
        d_gu = scatter_rep(scatter_far(gu_x, size), rep)
        d_out = scatter_rep(scatter_far(scatter_pair(out_core, size, 2, 1), size), rep)
        d_qkv = scatter_pair(scatter_begin(d_qkv, size), size, 1, 2)
        d_qkv = scatter_rep(scatter_far(scatter_pair(d_qkv, size, 2, 1), size), rep)
        owned = [
            d_qkv[:, :D],
            d_qkv[:, D : D + KV_W],
            d_qkv[:, D + KV_W :],
            d_out,
            d_gu[:, :FF],
            d_gu[:, FF:],
            d_down,
        ]
        owned = [w.reshape(-1) for w in owned]
        gains = sum_small(jnp.stack([g1, g2]), size, rep)
    else:
        terms = [
            d_qkv[:, :D], d_qkv[:, D : D + KV_W], d_qkv[:, D + KV_W :], d_out, d_gate, d_up, d_down
        ]
        owned = []
        for term in terms:
            mine = lax.psum_scatter(term.reshape(-1), "dp", scatter_dimension=0, tiled=True)
            owned.append(lax.psum(mine.astype(BF16), "rep").astype(F32))
        gains = lax.psum(jnp.stack([g1, g2]), ("dp", "rep"))
    return (
        result.reshape(seqs, SEQ, D),
        grad_hidden.reshape(seqs, SEQ, D),
        gains[0],
        *owned[:4],
        gains[1],
        *owned[4:],
    )


def solution(mesh):
    flat = P("dp")
    seqs = P(("dp", "rep"), None, None)
    return jax.shard_map(
        functools.partial(per_device, mesh.shape["dp"], mesh.shape["rep"]),
        mesh=mesh,
        in_specs=(
            seqs,
            P(("dp", "rep"), None),
            P(),
            flat,
            flat,
            flat,
            flat,
            P(),
            flat,
            flat,
            flat,
            seqs,
        ),
        out_specs=(seqs, seqs, P(), flat, flat, flat, flat, P(), flat, flat, flat),
        check_vma=False,
    )
```

profile of v0, /device:TPU:0, one launch (start us, length us, event | category | flops | bytes accessed | tf_op | source)
XLA Modules:
  0.0 427.9 jit_solution(8993356193594387509)
XLA Ops:
  4.2 5.1 %collective-permute-start = (bf16[36,1536]{1,0:T(8,128)(2,1)S(1)}, bf16[36,1536]{1,0:T(8,128)(2,1)S(1)}, u32[]{:S(2)}, u32[]{:S(2)}) collective-permute-start(bf16[36,1536]{1,0:T(8,128)(2,1)S(1)} %concatenate.16), channel_id=1, source_target_pairs={{0,24},{2,26},{4,28},{6,30},{8,16},{10,18},{12,20},{14,22},{16,8},... | collective-permute-start | bytes 331784 | tf_op jit(solution)/shard_map/ppermute | solution.py:178
  10.0 4.5 %convert_bitcast_fusion = f32[4,72,8,512]{3,2,1,0:T(8,128)} fusion(bf16[4,512,576]{1,2,0:T(8,128)(2,1)} %param.12), kind=kLoop, calls=%fused_computation.5 | loop fusion | flops 1179648 | bytes 7077888
  17.3 5.3 %copy.140 = f32[4,72,8,512]{3,2,0,1:T(8,128)} copy(f32[4,72,8,512]{3,2,1,0:T(8,128)} %convert_bitcast_fusion) | data formatting | bytes 9437184 | tf_op jit(solution)/shard_map/convert_element_type | solution.py:305
  23.7 1.8 copy.141
  26.6 3.8 collective-permute-start.5
  31.1 1.7 collective-permute-start.3
  32.8 4.6 %collective-permute-done.5 = bf16[36,3072]{1,0:T(8,128)(2,1)S(1)} collective-permute-done((bf16[36,3072]{1,0:T(8,128)(2,1)S(1)}, bf16[36,3072]{1,0:T(8,128)(2,1)S(1)}, u32[]{:S(2)}, u32[]{:S(2)}) %collective-permute-start.5) | collective-permute-done | bytes 221216 | tf_op jit(solution)/shard_map/ppermute | solution.py:178
  37.4 13.0 %collective-permute-done.6 = bf16[36,3072]{1,0:T(8,128)(2,1)S(1)} collective-permute-done((bf16[36,3072]{1,0:T(8,128)(2,1)S(1)}, bf16[36,3072]{1,0:T(8,128)(2,1)S(1)}, u32[]{:S(2)}, u32[]{:S(2)}) %collective-permute-start.6) | collective-permute-done | bytes 221216 | tf_op jit(solution)/shard_map/ppermute | solution.py:178
  50.7 2.4 collective-permute-start.9
  56.4 4.5 %collective-permute-done.10 = bf16[96,576]{1,0:T(8,128)(2,1)S(1)} collective-permute-done((bf16[96,576]{1,0:T(8,128)(2,1)S(1)}, bf16[96,576]{1,0:T(8,128)(2,1)S(1)}, u32[]{:S(2)}, u32[]{:S(2)}) %collective-permute-start.10) | collective-permute-done | bytes 110624 | tf_op jit(solution)/shard_map/ppermute | solution.py:178
  63.9 21.2 %collective-permute-done.13 = bf16[4,96,576]{2,1,0:T(8,128)(2,1)S(1)} collective-permute-done((bf16[4,96,576]{2,1,0:T(8,128)(2,1)S(1)}, bf16[4,96,576]{2,1,0:T(8,128)(2,1)S(1)}, u32[]{:S(2)}, u32[]{:S(2)}) %collective-permute-start.13) | collective-permute-done | bytes 442400 | tf_op jit(solution)/shard_map/ppermute | solution.py:178
  88.5 2.6 copy.108
  93.6 4.0 reshape.200
  97.6 9.3 %fusion.16.qkv_ref = f32[960,2048]{1,0:T(8,128)} fusion(bf16[576,1536]{1,0:T(8,128)(2,1)} %reshape.200, f32[2048,576]{0,1:T(8,128)} %bitcast.195, f32[576]{0:T(1024)S(1)} %convert_element_type.280, f32[2048]{0:T(1024)S(1)} %bitcast.224), kind=kOutput, calls=%fused_computation.56 | convolution fusion | flops 2268463104 | bytes 13773056 | tf_op jit(solution)/shard_map/dot_general | solution.py:33
  106.9 13.0 %attend_forward.2 = (bf16[2,9,768,256]{3,2,1,0:T(8,128)(2,1)S(1)}, bf16[576,2048]{1,0:T(8,128)(2,1)S(1)}, bf16[576,1024]{1,0:T(8,128)(2,1)S(1)}, bf16[192,1024]{1,0:T(8,128)(2,1)S(1)}, bf16[192,1024]{1,0:T(8,128)(2,1)S(1)}) custom-call(f32[960,2048]{1,0:T(8,128)} %fusion.16.qkv_ref, f32[64,2048]{1,0:T(8,128)S(1)} %get-tuple-element.166.cos_ref, ...), custom_call_target="tpu_custom_call" | custom-call | flops 10000000000 | bytes 16000000 | tf_op jit(solution)/shard_map/attend_forward/pallas_call | solution.py:76
  119.9 2.8 copy-done.8
  122.8 13.7 %attend_forward.3 = (bf16[2,9,768,256]{3,2,1,0:T(8,128)(2,1)S(1)}, bf16[576,2048]{1,0:T(8,128)(2,1)S(1)}, bf16[576,1024]{1,0:T(8,128)(2,1)S(1)}, bf16[192,1024]{1,0:T(8,128)(2,1)S(1)}, bf16[192,1024]{1,0:T(8,128)(2,1)S(1)}) custom-call(f32[960,2048]{1,0:T(8,128)} %fusion.16.qkv_ref, ...), custom_call_target="tpu_custom_call", output_to_operand_aliasing={{1}: (6, {})} | custom-call | flops 10000000000 | bytes 16000000 | tf_op jit(solution)/shard_map/attend_forward/pallas_call | solution.py:76
  136.6 4.1 multiply_reduce_fusion.4
  140.8 1.9 multiply_convert_fusion.3
  146.9 2.7 select_bitcast_fusion.1
  150.0 2.2 copy.111
  152.1 4.9 %reshape.204 = bf16[576,3072]{1,0:T(8,128)(2,1)} reshape(bf16[4,2,2,36,3072]{4,3,2,1,0:T(8,128)(2,1)} %copy.111) | data formatting | bytes 7077888 | tf_op jit(solution)/shard_map/reshape | solution.py:205
  157.0 9.9 %fusion.9 = f32[2048,1536]{1,0:T(8,128)} fusion(bf16[2048,576]{0,1:T(8,128)(2,1)S(1)} %copy-done.40, bf16[576,3072]{1,0:T(8,128)(2,1)} %reshape.204), kind=kOutput, calls=%fused_computation.46 | convolution fusion | flops 3623878656 | bytes 16711680 | tf_op jit(solution)/shard_map/dot_general | solution.py:33
  166.9 13.3 %multiply_convert_fusion.2 = (bf16[2048,1536]{1,0:T(8,128)(2,1)}, f32[2048,1536]{1,0:T(8,128)}) fusion(f32[2048,1536]{1,0:T(8,128)} %fusion.9, bf16[2048,576]{0,1:T(8,128)(2,1)S(1)} %copy-done.40, bf16[576,3072]{1,0:T(8,128)(2,1)S(1)} %copy-done.35), kind=kOutput, calls=%fused_computation.2 | convolution fusion | flops 3642753024 | bytes 35586048 | tf_op jit(solution)/shard_map/dot_general | solution.py:33
  180.2 8.4 %add_convert_fusion.1 = bf16[2048,576]{0,1:T(8,128)(2,1)} fusion(f32[2048,576]{0,1:T(8,128)S(1)} %bitcast.205, bf16[2048,1536]{1,0:T(8,128)(2,1)} %get-tuple-element.162, bf16[1536,576]{1,0:T(8,128)(2,1)S(1)} %bitcast.220), kind=kOutput, calls=%fused_computation.13 | convolution fusion | flops 3626237952 | bytes 15138816 | tf_op jit(solution)/shard_map/dot_general | solution.py:33
  188.6 7.7 %convolution_convert_fusion = bf16[1536,576]{0,1:T(8,128)(2,1)} fusion(bf16[2048,576]{0,1:T(8,128)(2,1)S(1)} %bitcast.208, bf16[2048,1536]{1,0:T(8,128)(2,1)} %get-tuple-element.162), kind=kOutput, calls=%fused_computation.24 | convolution fusion | flops 3624763392 | bytes 10420224 | tf_op jit(solution)/shard_map/dot_general | solution.py:33
  196.3 17.6 %multiply_convert_fusion.1 = (bf16[2048,1536]{1,0:T(8,128)(2,1)}, bf16[2048,1536]{1,0:T(8,128)(2,1)}) fusion(f32[2048,1536]{1,0:T(8,128)} %fusion.9, f32[2048,1536]{1,0:T(8,128)} %get-tuple-element.163, bf16[2048,576]{0,1:T(8,128)(2,1)S(1)} %bitcast.209, bf16[1536,576]{1,0:T(8,128)(2,1)} %bitcast.219), kind=kOutput, calls=%fused_computation.1 | convolution fusion | flops 3664773120 | bytes 41877504 | tf_op jit(solution)/shard_map/dot_general | solution.py:33
  213.9 8.6 %convolution_convert_fusion.2 = bf16[576,1536]{1,0:T(8,128)(2,1)} fusion(bf16[2048,576]{0,1:T(8,128)(2,1)} %multiply_convert_fusion.3, bf16[2048,1536]{1,0:T(8,128)(2,1)} %get-tuple-element.40), kind=kOutput, calls=%fused_computation.26 | convolution fusion | flops 3624763392 | bytes 10420224 | tf_op jit(solution)/shard_map/dot_general | solution.py:33
  222.5 2.7 copy.114
  226.9 6.7 %convolution_convert_fusion.3 = bf16[576,1536]{1,0:T(8,128)(2,1)S(1)} fusion(bf16[2048,576]{0,1:T(8,128)(2,1)S(1)} %copy-done.41, bf16[2048,1536]{1,0:T(8,128)(2,1)} %get-tuple-element.39), kind=kOutput, calls=%fused_computation.27 | convolution fusion | flops 3624763392 | bytes 10420224 | tf_op jit(solution)/shard_map/dot_general | solution.py:33
  235.8 2.3 pad_maximum_fusion
  239.4 6.8 %fusion.7 = f32[2048,576]{0,1:T(8,128)S(1)} fusion(bf16[2048,1536]{1,0:T(8,128)(2,1)} %get-tuple-element.39, bf16[576,3072]{1,0:T(8,128)(2,1)S(1)} %copy-done.36), kind=kOutput, calls=%fused_computation.44 | convolution fusion | flops 3623878656 | bytes 12779520 | tf_op jit(solution)/shard_map/dot_general | solution.py:33
  246.2 7.0 %multiply_reduce_fusion = (f32[576]{0:T(1024)}, f32[2048]{0:T(1024)S(1)}, f32[2048,576]{0,1:T(8,128)}) fusion(f32[2048,576]{0,1:T(8,128)S(1)} %bitcast.207, f32[2048]{0:T(1024)S(1)} %add_rsqrt_fusion, f32[576]{0:T(1024)S(1)} %convert_element_type.285, f32[2048,576]{0,1:T(8,128)S(1)} %fusion.7, bf16[2048,1536]{1,0:T(8,128)(2,1)S(1)} %bitcast.230, ...), kind=kOutput, calls=%fused_computation.7 | convolution fusion | flops 3632133632 | bytes 22239488 | tf_op jit(solution)/shard_map/dot_general | solution.py:33
  253.8 4.7 %reshape.209 = bf16[4,2,2,36,3072]{4,3,2,1,0:T(8,128)(2,1)} reshape(bf16[576,3072]{1,0:T(8,128)(2,1)} %pad_maximum_fusion) | data formatting | bytes 7077888 | tf_op jit(solution)/shard_map/reshape | solution.py:210
  258.5 3.9 dynamic-slice_bitcast_fusion
  262.4 2.6 copy.119
  265.0 4.1 multiply_add_fusion
  269.1 2.1 copy-done.20
  271.2 2.9 convolution_convert_fusion.5
  274.2 2.4 reshape.210
  280.9 6.1 %convolution_convert_fusion.1.do_ref = bf16[576,2048]{1,0:T(8,128)(2,1)} fusion(f32[2048,576]{0,1:T(8,128)} %copy-done.20, bf16[576,1536]{1,0:T(8,128)(2,1)} %reshape.200), kind=kOutput, calls=%fused_computation.25 | convolution fusion | flops 1361313792 | bytes 7815168 | tf_op jit(solution)/shard_map/dot_general | solution.py:33
  287.8 5.7 %collective-permute-done.19 = bf16[4,96,576]{2,1,0:T(8,128)(2,1)S(1)} collective-permute-done((bf16[4,96,576]{2,1,0:T(8,128)(2,1)S(1)}, bf16[4,96,576]{2,1,0:T(8,128)(2,1)S(1)}, u32[]{:S(2)}, u32[]{:S(2)}) %collective-permute-start.19) | collective-permute-done | bytes 442400 | tf_op jit(solution)/shard_map/ppermute | solution.py:178
  293.6 3.3 collective-permute-done.34
  297.0 1.8 collective-permute-start.37
  299.2 2.3 collective-permute-start.35
  301.5 1.8 collective-permute-start.22
  304.3 4.2 collective-permute-done.36
  310.1 5.0 %collective-permute-done.21 = bf16[96,576]{1,0:T(8,128)(2,1)S(1)} collective-permute-done((bf16[96,576]{1,0:T(8,128)(2,1)S(1)}, bf16[96,576]{1,0:T(8,128)(2,1)S(1)}, u32[]{:S(2)}, u32[]{:S(2)}) %collective-permute-start.21) | collective-permute-done | bytes 110624 | tf_op jit(solution)/shard_map/ppermute | solution.py:178
  321.8 1.7 convert_add_fusion.11
  323.5 1.8 reshape.222
  325.2 2.8 fusion.1
  330.7 13.4 %attend_backward.2.refs_3_ = bf16[960,2048]{1,0:T(8,128)(2,1)S(1)} custom-call(bf16[2,9,768,256]{3,2,1,0:T(8,128)(2,1)} %copy-done.8, bf16[576,2048]{1,0:T(8,128)(2,1)S(1)} %copy-done.1, bf16[576,2048]{1,0:T(8,128)(2,1)S(1)} %copy-done.6, bf16[576,1024]{1,0:T(8,128)(2,1)S(1)} %copy-done.10, bf16[192,1024]{1,0:T(8,128)(2,1)S(1)} %copy-done.16, ...), custom_call_target="tpu_custom_call" | custom-call | flops 20000000000 | bytes 16000000 | tf_op jit(solution)/shard_map/attend_backward/pallas_call | solution.py:152
  344.1 4.3 collective-permute-done.17
  348.9 14.1 %attend_backward.3 = bf16[960,2048]{1,0:T(8,128)(2,1)S(1)} custom-call(bf16[2,9,768,256]{3,2,1,0:T(8,128)(2,1)} %copy-done.7, bf16[576,2048]{1,0:T(8,128)(2,1)S(1)} %copy-done.1, bf16[576,2048]{1,0:T(8,128)(2,1)S(1)} %copy-done.6, bf16[576,1024]{1,0:T(8,128)(2,1)S(1)} %get-tuple-element.42.q_ref, ...), custom_call_target="tpu_custom_call", output_to_operand_aliasing={{}: (11, {})} | custom-call | flops 20000000000 | bytes 16000000 | tf_op jit(solution)/shard_map/attend_backward/pallas_call | solution.py:152
  363.0 4.7 %multiply_reduce_fusion.1 = (f32[576]{0:T(1024)S(1)}, f32[2048]{0:T(1024)S(1)}, f32[2048,576]{0,1:T(8,128)}) fusion(f32[2048,576]{0,1:T(8,128)S(1)} %bitcast.202, f32[2048]{0:T(1024)S(1)} %bitcast.225, f32[576]{0:T(1024)S(1)} %copy-done.52, bf16[960,2048]{1,0:T(8,128)(2,1)S(1)} %attend_backward.3, bf16[576,1536]{1,0:T(8,128)(2,1)S(1)} %copy-done.34), kind=kOutput, calls=%fused_computation.8 | convolution fusion | flops 2271999488 | bytes 14571776 | tf_op jit(solution)/shard_map/dot_general | solution.py:33
  367.8 2.6 convolution_convert_fusion.4
  374.9 3.0 collective-permute-done.25
  378.1 7.1 %add_convert_fusion = bf16[2048,576]{0,1:T(8,128)(2,1)S(1)} fusion(f32[2048,576]{0,1:T(8,128)} %copy-done.20, f32[2048,576]{0,1:T(8,128)} %get-tuple-element.165, f32[2048,576]{0,1:T(8,128)} %bitcast.196, f32[2048]{0:T(1024)S(1)} %broadcast_multiply_fusion, f32[576]{0:T(1024)S(1)} %copy-done.53, f32[2048]{0:T(1024)S(1)} %bitcast.227), kind=kLoop, calls=%fused_computation.9 | loop fusion | flops 9437184 | bytes 16533760 | tf_op jit(solution)/shard_map/convert_element_type | solution.py:360
  388.3 2.1 collective-permute-start.41
  395.2 3.9 collective-permute-done.41
  399.1 12.0 %collective-permute-done.40 = bf16[36,3072]{1,0:T(8,128)(2,1)S(1)} collective-permute-done((bf16[36,3072]{1,0:T(8,128)(2,1)S(1)}, bf16[36,3072]{1,0:T(8,128)(2,1)S(1)}, u32[]{:S(2)}, u32[]{:S(2)}) %collective-permute-start.40) | collective-permute-done | bytes 221216 | tf_op jit(solution)/shard_map/ppermute | solution.py:178
  412.1 2.2 collective-permute-start.32
  414.2 2.3 collective-permute-start.30
  418.5 2.1 collective-permute-done.31
  (305 shorter events, 72.6 us)
Async XLA Ops:
  4.2 21.3 %collective-permute-start = (bf16[36,1536]{1,0:T(8,128)(2,1)S(1)}, bf16[36,1536]{1,0:T(8,128)(2,1)S(1)}, u32[]{:S(2)}, u32[]{:S(2)}) collective-permute-start(bf16[36,1536]{1,0:T(8,128)(2,1)S(1)} %concatenate.16), channel_id=1, source_target_pairs={{0,24},{2,26},{4,28},{6,30},{8,16},{10,18},{12,20},{14,22},{16,8},... | collective-permute-start | bytes 331784 | tf_op jit(solution)/shard_map/ppermute | solution.py:178
  9.3 16.1 %collective-permute-start.1 = (bf16[36,1536]{1,0:T(8,128)(2,1)S(1)}, bf16[36,1536]{1,0:T(8,128)(2,1)}, u32[]{:S(2)}, u32[]{:S(2)}) collective-permute-start(bf16[36,1536]{1,0:T(8,128)(2,1)S(1)} %concatenate.16), channel_id=1, source_target_pairs={{0,16},{2,18},{4,20},{6,22},{8,24},{10,26},{12,28},{14,30},{16,0},... | collective-permute-start | bytes 331784 | tf_op jit(solution)/shard_map/ppermute | solution.py:178
  9.3 16.1 %collective-permute-start.2 = (bf16[36,1536]{1,0:T(8,128)(2,1)S(1)}, bf16[36,1536]{1,0:T(8,128)(2,1)}, u32[]{:S(2)}, u32[]{:S(2)}) collective-permute-start(bf16[36,1536]{1,0:T(8,128)(2,1)S(1)} %concatenate.16), channel_id=1, source_target_pairs={{0,8},{2,10},{4,12},{6,14},{8,0},{10,2},{12,4},{14,6},{16,24},{18,... | collective-permute-start | bytes 331784 | tf_op jit(solution)/shard_map/ppermute | solution.py:178
  22.6 75.0 %copy-start.51 = (f32[576]{0:T(1024)}, f32[576]{0:T(1024)S(1)}, u32[]{:S(2)}) copy-start(f32[576]{0:T(1024)S(1)} %convert_element_type.280) | copy-start | bytes 6916
  22.6 75.0 %copy-start.46 = (f32[1,4,4,128]{3,1,2,0:T(4,128)}, f32[1,4,4,128]{3,1,2,0:T(4,128)S(1)}, u32[]{:S(2)}) copy-start(f32[1,4,4,128]{3,1,2,0:T(4,128)S(1)} %copy.142) | copy-start | bytes 24580
  26.6 10.9 %collective-permute-start.5 = (bf16[36,3072]{1,0:T(8,128)(2,1)S(1)}, bf16[36,3072]{1,0:T(8,128)(2,1)S(1)}, u32[]{:S(2)}, u32[]{:S(2)}) collective-permute-start(bf16[36,3072]{1,0:T(8,128)(2,1)S(1)} %pad_maximum_fusion.9), channel_id=1, source_target_pairs={{0,24},{2,26},{4,28},{6,30},{8,16},{10,18},{12,20},{14,22},{16,8},... | collective-permute-start | bytes 663560 | tf_op jit(solution)/shard_map/ppermute | solution.py:178
  30.4 20.0 %collective-permute-start.6 = (bf16[36,3072]{1,0:T(8,128)(2,1)S(1)}, bf16[36,3072]{1,0:T(8,128)(2,1)S(1)}, u32[]{:S(2)}, u32[]{:S(2)}) collective-permute-start(bf16[36,3072]{1,0:T(8,128)(2,1)S(1)} %pad_maximum_fusion.9), channel_id=1, source_target_pairs={{0,16},{2,18},{4,20},{6,22},{8,24},{10,26},{12,28},{14,30},{16,0},... | collective-permute-start | bytes 663560 | tf_op jit(solution)/shard_map/ppermute | solution.py:178
  30.4 20.0 %collective-permute-start.7 = (bf16[36,3072]{1,0:T(8,128)(2,1)S(1)}, bf16[36,3072]{1,0:T(8,128)(2,1)S(1)}, u32[]{:S(2)}, u32[]{:S(2)}) collective-permute-start(bf16[36,3072]{1,0:T(8,128)(2,1)S(1)} %pad_maximum_fusion.9), channel_id=1, source_target_pairs={{0,8},{2,10},{4,12},{6,14},{8,0},{10,2},{12,4},{14,6},{16,24},{18,... | collective-permute-start | bytes 663560 | tf_op jit(solution)/shard_map/ppermute | solution.py:178
  31.1 91.6 %copy-start.2 = (f32[64,2048]{1,0:T(8,128)}, f32[64,2048]{1,0:T(8,128)S(1)}, u32[]{:S(2)}) copy-start(f32[64,2048]{1,0:T(8,128)S(1)} %get-tuple-element.166.cos_ref) | copy-start | bytes 1572868
  31.1 91.6 %copy-start.4 = (f32[64,2048]{1,0:T(8,128)}, f32[64,2048]{1,0:T(8,128)S(1)}, u32[]{:S(2)}) copy-start(f32[64,2048]{1,0:T(8,128)S(1)} %get-tuple-element.167.sin_ref) | copy-start | bytes 1572868
  31.1 32.1 %collective-permute-start.3 = (bf16[4,36,1536]{2,1,0:T(8,128)(2,1)S(1)}, bf16[4,36,1536]{2,1,0:T(8,128)(2,1)S(1)}, u32[]{:S(2)}, u32[]{:S(2)}) collective-permute-start(bf16[4,36,1536]{2,1,0:T(8,128)(2,1)S(1)} %pad_maximum_fusion.7), channel_id=1, source_target_pairs={{0,4},{2,6},{4,0},{6,2},{8,12},{10,14},{12,8},{14,10},{16,20},{18,... | collective-permute-start | bytes 1327112 | tf_op jit(solution)/shard_map/ppermute | solution.py:178
  50.6 10.3 %collective-permute-start.10 = (bf16[96,576]{1,0:T(8,128)(2,1)S(1)}, bf16[96,576]{1,0:T(8,128)(2,1)S(1)}, u32[]{:S(2)}, u32[]{:S(2)}) collective-permute-start(bf16[96,576]{1,0:T(8,128)(2,1)S(1)} %reshape.202), channel_id=1, source_target_pairs={{0,16},{2,18},{4,20},{6,22},{8,24},{10,26},{12,28},{14,30},{16,0},... | collective-permute-start | bytes 331784 | tf_op jit(solution)/shard_map/ppermute | solution.py:178
  50.7 10.2 %collective-permute-start.9 = (bf16[96,576]{1,0:T(8,128)(2,1)S(1)}, bf16[96,576]{1,0:T(8,128)(2,1)S(1)}, u32[]{:S(2)}, u32[]{:S(2)}) collective-permute-start(bf16[96,576]{1,0:T(8,128)(2,1)S(1)} %reshape.202), channel_id=1, source_target_pairs={{0,24},{2,26},{4,28},{6,30},{8,16},{10,18},{12,20},{14,22},{16,8},... | collective-permute-start | bytes 331784 | tf_op jit(solution)/shard_map/ppermute | solution.py:178
  53.1 8.3 %collective-permute-start.11 = (bf16[96,576]{1,0:T(8,128)(2,1)S(1)}, bf16[96,576]{1,0:T(8,128)(2,1)S(1)}, u32[]{:S(2)}, u32[]{:S(2)}) collective-permute-start(bf16[96,576]{1,0:T(8,128)(2,1)S(1)} %reshape.202), channel_id=1, source_target_pairs={{0,8},{2,10},{4,12},{6,14},{8,0},{10,2},{12,4},{14,6},{16,24},{18,... | collective-permute-start | bytes 331784 | tf_op jit(solution)/shard_map/ppermute | solution.py:178
  54.9 31.8 %collective-permute-start.8 = (bf16[4,36,3072]{2,0,1:T(4,128)(2,1)S(1)}, bf16[4,36,3072]{2,0,1:T(4,128)(2,1)S(1)}, u32[]{:S(2)}, u32[]{:S(2)}) collective-permute-start(bf16[4,36,3072]{2,0,1:T(4,128)(2,1)S(1)} %copy.105), channel_id=1, source_target_pairs={{0,4},{2,6},{4,0},{6,2},{8,12},{10,14},{12,8},{14,10},{16,20},{18,... | collective-permute-start | bytes 2654216 | tf_op jit(solution)/shard_map/ppermute | solution.py:178
  61.7 23.5 %collective-permute-start.13 = (bf16[4,96,576]{2,1,0:T(8,128)(2,1)S(1)}, bf16[4,96,576]{2,1,0:T(8,128)(2,1)S(1)}, u32[]{:S(2)}, u32[]{:S(2)}) collective-permute-start(bf16[4,96,576]{2,1,0:T(8,128)(2,1)S(1)} %pad_maximum_fusion.8), channel_id=1, source_target_pairs={{0,4},{2,6},{4,0},{6,2},{8,12},{10,14},{12,8},{14,10},{16,20},{18,... | collective-permute-start | bytes 1327112 | tf_op jit(solution)/shard_map/ppermute | solution.py:178
  63.9 27.7 %collective-permute-start.4 = (bf16[2,4,36,1536]{3,1,2,0:T(4,128)(2,1)S(1)}, bf16[2,4,36,1536]{3,1,2,0:T(4,128)(2,1)S(1)}, u32[]{:S(2)}, u32[]{:S(2)}) collective-permute-start(bf16[2,4,36,1536]{3,1,2,0:T(4,128)(2,1)S(1)} %copy.101), channel_id=1, source_target_pairs={{0,2},{2,0},{4,6},{6,4},{8,10},{10,8},{12,14},{14,12},{16,18},{18,... | collective-permute-start | bytes 2654216 | tf_op jit(solution)/shard_map/ppermute | solution.py:178
  86.6 56.9 %collective-permute-start.14 = (bf16[2,4,96,576]{3,2,1,0:T(8,128)(2,1)}, bf16[2,4,96,576]{3,2,1,0:T(8,128)(2,1)}, u32[]{:S(2)}, u32[]{:S(2)}) collective-permute-start(bf16[2,4,96,576]{3,2,1,0:T(8,128)(2,1)} %pad_maximum_fusion.4), channel_id=1, source_target_pairs={{0,2},{2,0},{4,6},{6,4},{8,10},{10,8},{12,14},{14,12},{16,18},{18,... | collective-permute-start | bytes 2654216 | tf_op jit(solution)/shard_map/ppermute | solution.py:178
  91.1 55.8 %collective-permute-start.12 = (bf16[2,4,36,3072]{3,1,2,0:T(4,128)(2,1)}, bf16[2,4,36,3072]{3,1,2,0:T(4,128)(2,1)}, u32[]{:S(2)}, u32[]{:S(2)}) collective-permute-start(bf16[2,4,36,3072]{3,1,2,0:T(4,128)(2,1)} %copy.108), channel_id=1, source_target_pairs={{0,2},{2,0},{4,6},{6,4},{8,10},{10,8},{12,14},{14,12},{16,18},{18,... | collective-permute-start | bytes 5308424 | tf_op jit(solution)/shard_map/ppermute | solution.py:178
  106.9 29.6 %slice-start = ((s8[4718592]{0:T(1024)(128)(4,1)}), s8[4194304]{0:T(1024)(128)(4,1)S(1)}, s32[]{:S(2)}) async-start(s8[4718592]{0:T(1024)(128)(4,1)} %bitcast.197), calls=%async_computation | async-start | bytes 8388608
  122.8 13.7 %copy-start.9 = (bf16[576,1024]{1,0:T(8,128)(2,1)}, bf16[576,1024]{1,0:T(8,128)(2,1)S(1)}, u32[]{:S(2)}) copy-start(bf16[576,1024]{1,0:T(8,128)(2,1)S(1)} %get-tuple-element.48.q_ref) | copy-start | bytes 3538948
  122.8 13.7 %copy-start.15 = (bf16[192,1024]{1,0:T(8,128)(2,1)}, bf16[192,1024]{1,0:T(8,128)(2,1)S(1)}, u32[]{:S(2)}) copy-start(bf16[192,1024]{1,0:T(8,128)(2,1)S(1)} %get-tuple-element.49.k_ref) | copy-start | bytes 1179652
  122.8 13.7 %copy-start.17 = (bf16[192,1024]{1,0:T(8,128)(2,1)}, bf16[192,1024]{1,0:T(8,128)(2,1)S(1)}, u32[]{:S(2)}) copy-start(bf16[192,1024]{1,0:T(8,128)(2,1)S(1)} %get-tuple-element.50.v_ref) | copy-start | bytes 1179652
  122.8 13.8 %slice-start.1 = ((s8[4718592]{0:T(1024)(128)(4,1)}), s8[524288]{0:T(1024)(128)(4,1)S(1)}, s32[]{:S(2)}) async-start(s8[4718592]{0:T(1024)(128)(4,1)} %bitcast.197), calls=%async_computation.1 | async-start | bytes 1048576
  157.0 23.2 %slice-start.4 = ((s8[4718592]{0:T(1024)(128)(4,1)}), s8[4194304]{0:T(1024)(128)(4,1)S(1)}, s32[]{:S(2)}) async-start(s8[4718592]{0:T(1024)(128)(4,1)} %bitcast.204), calls=%async_computation.4 | async-start | bytes 8388608
  166.9 13.3 %slice-start.5 = ((s8[4718592]{0:T(1024)(128)(4,1)}), s8[524288]{0:T(1024)(128)(4,1)S(1)}, s32[]{:S(2)}) async-start(s8[4718592]{0:T(1024)(128)(4,1)} %bitcast.204), calls=%async_computation.5 | async-start | bytes 1048576
  166.9 13.3 %copy-start.42 = (bf16[4,2,2,96,576]{4,3,2,1,0:T(8,128)(2,1)S(1)}, bf16[4,2,2,96,576]{4,3,2,1,0:T(8,128)(2,1)}, u32[]{:S(2)}) copy-start(bf16[4,2,2,96,576]{4,3,2,1,0:T(8,128)(2,1)} %copy.112) | copy-start | bytes 5308420
  225.6 12.5 %collective-permute-start.15 = (bf16[4,2,96,576]{3,2,0,1:T(8,128)(2,1)S(1)}, bf16[4,2,96,576]{3,2,0,1:T(8,128)(2,1)S(1)}, u32[]{:S(2)}, u32[]{:S(2)}) collective-permute-start(bf16[4,2,96,576]{3,2,0,1:T(8,128)(2,1)S(1)} %bitcast.222), channel_id=1, source_target_pairs={{0,2},{2,0},{4,6},{6,4},{8,10},{10,8},{12,14},{14,12},{16,18},{18,... | collective-permute-start | bytes 2654216 | tf_op jit(solution)/shard_map/ppermute | solution.py:178
  265.0 60.2 %collective-permute-start.16 = (bf16[4,2,36,3072]{3,0,2,1:T(4,128)(2,1)}, bf16[4,2,36,3072]{3,0,2,1:T(4,128)(2,1)}, u32[]{:S(2)}, u32[]{:S(2)}) collective-permute-start(bf16[4,2,36,3072]{3,0,2,1:T(4,128)(2,1)} %copy.119), channel_id=1, source_target_pairs={{0,2},{2,0},{4,6},{6,4},{8,10},{10,8},{12,14},{14,12},{16,18},{18,... | collective-permute-start | bytes 5308424 | tf_op jit(solution)/shard_map/ppermute | solution.py:178
  277.7 9.4 %collective-permute-start.18 = (bf16[4,2,36,576]{3,2,1,0:T(8,128)(2,1)S(1)}, bf16[4,2,36,576]{3,2,1,0:T(8,128)(2,1)S(1)}, u32[]{:S(2)}, u32[]{:S(2)}) collective-permute-start(bf16[4,2,36,576]{3,2,1,0:T(8,128)(2,1)S(1)} %dynamic-slice_bitcast_fusion.3), channel_id=1, source_target_pairs={{0,2},{2,0},{4,6},{6,4},{8,10},{10,8},{12,14},{14,12},{16,18},{18,... | collective-permute-start | bytes 995336 | tf_op jit(solution)/shard_map/ppermute | solution.py:178
  279.3 14.2 %collective-permute-start.19 = (bf16[4,96,576]{2,1,0:T(8,128)(2,1)S(1)}, bf16[4,96,576]{2,1,0:T(8,128)(2,1)S(1)}, u32[]{:S(2)}, u32[]{:S(2)}) collective-permute-start(bf16[4,96,576]{2,1,0:T(8,128)(2,1)S(1)} %dynamic-slice_bitcast_fusion.2), channel_id=1, source_target_pairs={{0,4},{2,6},{4,0},{6,2},{8,12},{10,14},{12,8},{14,10},{16,20},{18,... | collective-permute-start | bytes 1327112 | tf_op jit(solution)/shard_map/ppermute | solution.py:178
  287.2 9.7 %collective-permute-start.34 = (bf16[4,36,576]{2,1,0:T(8,128)(2,1)S(1)}, bf16[4,36,576]{2,1,0:T(8,128)(2,1)S(1)}, u32[]{:S(2)}, u32[]{:S(2)}) collective-permute-start(bf16[4,36,576]{2,1,0:T(8,128)(2,1)S(1)} %dynamic-slice_bitcast_fusion.8), channel_id=1, source_target_pairs={{0,4},{2,6},{4,0},{6,2},{8,12},{10,14},{12,8},{14,10},{16,20},{18,... | collective-permute-start | bytes 497672 | tf_op jit(solution)/shard_map/ppermute | solution.py:178
  297.0 6.6 %collective-permute-start.37 = (bf16[36,576]{1,0:T(8,128)(2,1)S(1)}, bf16[36,576]{1,0:T(8,128)(2,1)S(1)}, u32[]{:S(2)}, u32[]{:S(2)}) collective-permute-start(bf16[36,576]{1,0:T(8,128)(2,1)S(1)} %get-tuple-element.154), channel_id=1, source_target_pairs={{0,24},{2,26},{4,28},{6,30},{8,16},{10,18},{12,20},{14,22},{16,8},... | collective-permute-start | bytes 124424 | tf_op jit(solution)/shard_map/ppermute | solution.py:178
  298.8 9.7 %collective-permute-start.36 = (bf16[36,576]{1,0:T(8,128)(2,1)S(1)}, bf16[36,576]{1,0:T(8,128)(2,1)S(1)}, u32[]{:S(2)}, u32[]{:S(2)}) collective-permute-start(bf16[36,576]{1,0:T(8,128)(2,1)S(1)} %get-tuple-element.155), channel_id=1, source_target_pairs={{0,16},{2,18},{4,20},{6,22},{8,24},{10,26},{12,28},{14,30},{16,0},... | collective-permute-start | bytes 124424 | tf_op jit(solution)/shard_map/ppermute | solution.py:178
  299.2 9.3 %collective-permute-start.35 = (bf16[36,576]{1,0:T(8,128)(2,1)S(1)}, bf16[36,576]{1,0:T(8,128)(2,1)S(1)}, u32[]{:S(2)}, u32[]{:S(2)}) collective-permute-start(bf16[36,576]{1,0:T(8,128)(2,1)S(1)} %get-tuple-element.153), channel_id=1, source_target_pairs={{0,8},{2,10},{4,12},{6,14},{8,0},{10,2},{12,4},{14,6},{16,24},{18,... | collective-permute-start | bytes 124424 | tf_op jit(solution)/shard_map/ppermute | solution.py:178
  301.5 8.6 %collective-permute-start.22 = (bf16[96,576]{1,0:T(8,128)(2,1)S(1)}, bf16[96,576]{1,0:T(8,128)(2,1)S(1)}, u32[]{:S(2)}, u32[]{:S(2)}) collective-permute-start(bf16[96,576]{1,0:T(8,128)(2,1)S(1)} %get-tuple-element.140), channel_id=1, source_target_pairs={{0,24},{2,26},{4,28},{6,30},{8,16},{10,18},{12,20},{14,22},{16,8},... | collective-permute-start | bytes 331784 | tf_op jit(solution)/shard_map/ppermute | solution.py:178
  303.6 11.5 %collective-permute-start.21 = (bf16[96,576]{1,0:T(8,128)(2,1)S(1)}, bf16[96,576]{1,0:T(8,128)(2,1)S(1)}, u32[]{:S(2)}, u32[]{:S(2)}) collective-permute-start(bf16[96,576]{1,0:T(8,128)(2,1)S(1)} %get-tuple-element.141), channel_id=1, source_target_pairs={{0,16},{2,18},{4,20},{6,22},{8,24},{10,26},{12,28},{14,30},{16,0},... | collective-permute-start | bytes 331784 | tf_op jit(solution)/shard_map/ppermute | solution.py:178
  308.5 7.4 %collective-permute-start.20 = (bf16[96,576]{1,0:T(8,128)(2,1)S(1)}, bf16[96,576]{1,0:T(8,128)(2,1)S(1)}, u32[]{:S(2)}, u32[]{:S(2)}) collective-permute-start(bf16[96,576]{1,0:T(8,128)(2,1)S(1)} %get-tuple-element.139), channel_id=1, source_target_pairs={{0,8},{2,10},{4,12},{6,14},{8,0},{10,2},{12,4},{14,6},{16,24},{18,... | collective-permute-start | bytes 331784 | tf_op jit(solution)/shard_map/ppermute | solution.py:178
  308.5 10.3 %collective-permute-start.38 = (bf16[36,576]{1,0:T(8,128)(2,1)S(1)}, bf16[36,576]{1,0:T(8,128)(2,1)S(1)}, u32[]{:S(2)}, u32[]{:S(2)}) collective-permute-start(bf16[36,576]{1,0:T(8,128)(2,1)S(1)} %fusion.35), channel_id=1, source_target_pairs={{0,1},{1,0},{2,3},{3,2},{4,5},{5,4},{6,7},{7,6},{8,9},{9,8},{10,11... | collective-permute-start | bytes 124424 | tf_op jit(solution)/shard_map/ppermute | solution.py:178
  316.6 5.2 %collective-permute-start.43 = (bf16[96,576]{1,0:T(8,128)(2,1)}, bf16[96,576]{1,0:T(8,128)(2,1)}, u32[]{:S(2)}, u32[]{:S(2)}) collective-permute-start(bf16[96,576]{1,0:T(8,128)(2,1)} %fusion.29), channel_id=1, source_target_pairs={{0,1},{1,0},{2,3},{3,2},{4,5},{5,4},{6,7},{7,6},{8,9},{9,8},{10,11... | collective-permute-start | bytes 331784 | tf_op jit(solution)/shard_map/ppermute | solution.py:178
  329.0 19.4 %collective-permute-start.17 = (bf16[4,36,3072]{2,0,1:T(4,128)(2,1)S(1)}, bf16[4,36,3072]{2,0,1:T(4,128)(2,1)S(1)}, u32[]{:S(2)}, u32[]{:S(2)}) collective-permute-start(bf16[4,36,3072]{2,0,1:T(4,128)(2,1)S(1)} %bitcast.223), channel_id=1, source_target_pairs={{0,4},{2,6},{4,0},{6,2},{8,12},{10,14},{12,8},{14,10},{16,20},{18,... | collective-permute-start | bytes 2654216 | tf_op jit(solution)/shard_map/ppermute | solution.py:178
  330.6 18.2 %copy-start.12 = (bf16[192,1024]{1,0:T(8,128)(2,1)S(1)}, bf16[192,1024]{1,0:T(8,128)(2,1)}, u32[]{:S(2)}) copy-start(bf16[192,1024]{1,0:T(8,128)(2,1)} %copy-done.11) | copy-start | bytes 1179652
  330.7 18.2 %copy-start.14 = (bf16[192,1024]{1,0:T(8,128)(2,1)S(1)}, bf16[192,1024]{1,0:T(8,128)(2,1)}, u32[]{:S(2)}) copy-start(bf16[192,1024]{1,0:T(8,128)(2,1)} %copy-done.13) | copy-start | bytes 1179652
  330.7 32.3 %slice-start.2 = ((s8[4718592]{0:T(1024)(128)(4,1)}), s8[524288]{0:T(1024)(128)(4,1)S(1)}, s32[]{:S(2)}) async-start(s8[4718592]{0:T(1024)(128)(4,1)} %bitcast.200), calls=%async_computation.2 | async-start | bytes 1048576
  344.1 18.9 %slice-start.3 = ((s8[4718592]{0:T(1024)(128)(4,1)}), s8[4194304]{0:T(1024)(128)(4,1)S(1)}, s32[]{:S(2)}) async-start(s8[4718592]{0:T(1024)(128)(4,1)} %bitcast.200), calls=%async_computation.3 | async-start | bytes 8388608
  348.8 14.2 %copy-start.31 = (bf16[4,36,3072]{2,1,0:T(8,128)(2,1)}, bf16[4,36,3072]{2,1,0:T(8,128)(2,1)S(1)}, u32[]{:S(2)}) copy-start(bf16[4,36,3072]{2,1,0:T(8,128)(2,1)S(1)} %fusion.2) | copy-start | bytes 2654212
  348.8 14.2 %copy-start.34 = (bf16[576,1536]{1,0:T(8,128)(2,1)S(1)}, bf16[576,1536]{1,0:T(8,128)(2,1)}, u32[]{:S(2)}) copy-start(bf16[576,1536]{1,0:T(8,128)(2,1)} %reshape.200) | copy-start | bytes 5308420
  348.8 14.2 %copy-start.47 = (f32[1,4,4,128]{3,1,2,0:T(4,128)S(1)}, f32[1,4,4,128]{3,1,2,0:T(4,128)}, u32[]{:S(2)}) copy-start(f32[1,4,4,128]{3,1,2,0:T(4,128)} %copy-done.46) | copy-start | bytes 24580
  348.8 14.2 %copy-start.52 = (f32[576]{0:T(1024)S(1)}, f32[576]{0:T(1024)}, u32[]{:S(2)}) copy-start(f32[576]{0:T(1024)} %copy-done.51) | copy-start | bytes 6916
  367.7 2.8 collective-permute-start.23
  370.5 3.7 collective-permute-start.24
  374.2 3.7 collective-permute-start.25
  374.8 18.5 %collective-permute-start.28 = (bf16[4,2,36,960]{3,0,2,1:T(4,128)(2,1)S(1)}, bf16[4,2,36,960]{3,0,2,1:T(4,128)(2,1)S(1)}, u32[]{:S(2)}, u32[]{:S(2)}) collective-permute-start(bf16[4,2,36,960]{3,0,2,1:T(4,128)(2,1)S(1)} %copy.126), channel_id=1, source_target_pairs={{0,2},{2,0},{4,6},{6,4},{8,10},{10,8},{12,14},{14,12},{16,18},{18,... | collective-permute-start | bytes 1658888 | tf_op jit(solution)/shard_map/ppermute | solution.py:178
  377.9 7.3 %collective-permute-start.26 = (f32[2,576]{1,0:T(2,128)S(1)}, f32[2,576]{1,0:T(2,128)S(1)}, u32[]{:S(2)}, u32[]{:S(2)}) collective-permute-start(f32[2,576]{1,0:T(2,128)S(1)} %add.215), channel_id=1, source_target_pairs={{0,16},{2,18},{4,20},{6,22},{8,24},{10,26},{12,28},{14,30},{16,0},... | collective-permute-start | bytes 13832 | tf_op jit(solution)/shard_map/ppermute | solution.py:178
  385.2 7.4 %collective-permute-start.27 = (f32[2,576]{1,0:T(2,128)S(1)}, f32[2,576]{1,0:T(2,128)S(1)}, u32[]{:S(2)}, u32[]{:S(2)}) collective-permute-start(f32[2,576]{1,0:T(2,128)S(1)} %add.216), channel_id=1, source_target_pairs={{0,1},{1,0},{2,3},{3,2},{4,5},{5,4},{6,7},{7,6},{8,9},{9,8},{10,11... | collective-permute-start | bytes 13832 | tf_op jit(solution)/shard_map/ppermute | solution.py:178
  388.3 10.8 %collective-permute-start.41 = (bf16[36,3072]{1,0:T(8,128)(2,1)S(1)}, bf16[36,3072]{1,0:T(8,128)(2,1)S(1)}, u32[]{:S(2)}, u32[]{:S(2)}) collective-permute-start(bf16[36,3072]{1,0:T(8,128)(2,1)S(1)} %get-tuple-element.127), channel_id=1, source_target_pairs={{0,24},{2,26},{4,28},{6,30},{8,16},{10,18},{12,20},{14,22},{16,8},... | collective-permute-start | bytes 663560 | tf_op jit(solution)/shard_map/ppermute | solution.py:178
  390.4 20.6 %collective-permute-start.40 = (bf16[36,3072]{1,0:T(8,128)(2,1)S(1)}, bf16[36,3072]{1,0:T(8,128)(2,1)S(1)}, u32[]{:S(2)}, u32[]{:S(2)}) collective-permute-start(bf16[36,3072]{1,0:T(8,128)(2,1)S(1)} %get-tuple-element.128), channel_id=1, source_target_pairs={{0,16},{2,18},{4,20},{6,22},{8,24},{10,26},{12,28},{14,30},{16,0},... | collective-permute-start | bytes 663560 | tf_op jit(solution)/shard_map/ppermute | solution.py:178
  391.7 19.3 %collective-permute-start.39 = (bf16[36,3072]{1,0:T(8,128)(2,1)S(1)}, bf16[36,3072]{1,0:T(8,128)(2,1)S(1)}, u32[]{:S(2)}, u32[]{:S(2)}) collective-permute-start(bf16[36,3072]{1,0:T(8,128)(2,1)S(1)} %get-tuple-element.126), channel_id=1, source_target_pairs={{0,8},{2,10},{4,12},{6,14},{8,0},{10,2},{12,4},{14,6},{16,24},{18,... | collective-permute-start | bytes 663560 | tf_op jit(solution)/shard_map/ppermute | solution.py:178
  393.6 18.3 %collective-permute-start.29 = (bf16[4,36,960]{2,1,0:T(8,128)(2,1)S(1)}, bf16[4,36,960]{2,1,0:T(8,128)(2,1)S(1)}, u32[]{:S(2)}, u32[]{:S(2)}) collective-permute-start(bf16[4,36,960]{2,1,0:T(8,128)(2,1)S(1)} %dynamic-slice_bitcast_fusion.4), channel_id=1, source_target_pairs={{0,4},{2,6},{4,0},{6,2},{8,12},{10,14},{12,8},{14,10},{16,20},{18,... | collective-permute-start | bytes 829448 | tf_op jit(solution)/shard_map/ppermute | solution.py:178
  411.2 6.3 %collective-permute-start.42 = (bf16[36,3072]{1,0:T(8,128)(2,1)S(1)}, bf16[36,3072]{1,0:T(8,128)(2,1)S(1)}, u32[]{:S(2)}, u32[]{:S(2)}) collective-permute-start(bf16[36,3072]{1,0:T(8,128)(2,1)S(1)} %fusion.25), channel_id=1, source_target_pairs={{0,1},{1,0},{2,3},{3,2},{4,5},{5,4},{6,7},{7,6},{8,9},{9,8},{10,11... | collective-permute-start | bytes 663560 | tf_op jit(solution)/shard_map/ppermute | solution.py:178
  412.1 6.4 %collective-permute-start.32 = (bf16[36,960]{1,0:T(8,128)(2,1)S(1)}, bf16[36,960]{1,0:T(8,128)(2,1)S(1)}, u32[]{:S(2)}, u32[]{:S(2)}) collective-permute-start(bf16[36,960]{1,0:T(8,128)(2,1)S(1)} %get-tuple-element.151), channel_id=1, source_target_pairs={{0,24},{2,26},{4,28},{6,30},{8,16},{10,18},{12,20},{14,22},{16,8},... | collective-permute-start | bytes 207368 | tf_op jit(solution)/shard_map/ppermute | solution.py:178
  414.2 6.3 %collective-permute-start.31 = (bf16[36,960]{1,0:T(8,128)(2,1)S(1)}, bf16[36,960]{1,0:T(8,128)(2,1)S(1)}, u32[]{:S(2)}, u32[]{:S(2)}) collective-permute-start(bf16[36,960]{1,0:T(8,128)(2,1)S(1)} %get-tuple-element.152), channel_id=1, source_target_pairs={{0,16},{2,18},{4,20},{6,22},{8,24},{10,26},{12,28},{14,30},{16,0},... | collective-permute-start | bytes 207368 | tf_op jit(solution)/shard_map/ppermute | solution.py:178
  414.2 6.3 %collective-permute-start.30 = (bf16[36,960]{1,0:T(8,128)(2,1)S(1)}, bf16[36,960]{1,0:T(8,128)(2,1)S(1)}, u32[]{:S(2)}, u32[]{:S(2)}) collective-permute-start(bf16[36,960]{1,0:T(8,128)(2,1)S(1)} %get-tuple-element.150), channel_id=1, source_target_pairs={{0,8},{2,10},{4,12},{6,14},{8,0},{10,2},{12,4},{14,6},{16,24},{18,... | collective-permute-start | bytes 207368 | tf_op jit(solution)/shard_map/ppermute | solution.py:178
  420.6 4.5 %collective-permute-start.33 = (bf16[36,960]{1,0:T(8,128)(2,1)S(1)}, bf16[36,960]{1,0:T(8,128)(2,1)S(1)}, u32[]{:S(2)}, u32[]{:S(2)}) collective-permute-start(bf16[36,960]{1,0:T(8,128)(2,1)S(1)} %fusion.32), channel_id=1, source_target_pairs={{0,1},{1,0},{2,3},{3,2},{4,5},{5,4},{6,7},{7,6},{8,9},{9,8},{10,11... | collective-permute-start | bytes 207368 | tf_op jit(solution)/shard_map/ppermute | solution.py:178
  (47 other events, 251.8 us)
where the time goes:
time: 436 us; the launch traced here: 428 us
  matrix products  116 us (27%)
  waiting for transfers between devices  94 us (22%)
  local copies, waits for them, and re-layouts  71.2 us (16%)
  Pallas kernels  54.2 us (12%)
  starting transfers between devices  49.5 us (11%)
  other arithmetic  40.7 us (9%)
    dot_general x15, matrix products, dot(): lax.dot_general(a, b, (((ca,), (cb,)), ((), ())), preferred_element_type=...  116 us
    ppermute x44, waiting for transfers between devices, swap(): return lax.ppermute(x, axis, [(i, i ^ bit) for i in range(size)])  94 us
    ppermute x44, starting transfers between devices, swap(): return lax.ppermute(x, axis, [(i, i ^ bit) for i in range(size)])  49.5 us
    pallas_call x2, Pallas kernels, attend_backward(): pl.pallas_call(attend_back_kernel, grid=(seqs,), in_specs=[pl.BlockSpec((...  27.5 us
    pallas_call x2, Pallas kernels, attend_forward(): pl.pallas_call(attend_kernel, grid=(seqs,), in_specs=[col(QKV), col(HEAD_...  26.7 us
    squeeze x8, local copies, waits for them, and re-layouts, scatter_pair(): send = lax.dynamic_index_in_dim(held, 1 - side, axis, keepdims=False)  9.22 us
    reshape x2, local copies, waits for them, and re-layouts, gather_end(): return held.transpose(2, 1, 0, 3, 4).reshape(-1, held.shape[-1])  8.87 us
    unnamed x136, local copies, waits for them, and re-layouts  8.85 us
  transfers between devices with their start and end apart: 44, of which 21 were waited for; matrix products, arithmetic and copies ran while one was open for 23% of the time, Pallas kernels for 9%

commit v1 on v0

--- a/solution.py
+++ b/solution.py
@@ -264,28 +264,20 @@
             w.reshape(part, -1) for w in (w_query, w_key, w_value, w_out, w_gate, w_up)
         ]
         attn_far = gather_far(jnp.concatenate(mats[:4], axis=1), size)
-        mlp_block, attn_far = lax.optimization_barrier(
-            (jnp.concatenate(mats[4:], axis=1), attn_far)
+        attn_w = gather_end(gather_pair(gather_pair(attn_far, size, 2), size, 1))
+        mlp_block, down_block, attn_w = lax.optimization_barrier(
+            (jnp.concatenate(mats[4:], axis=1), w_down.reshape(FF // size, D), attn_w)
         )
         mlp_far = gather_far(mlp_block, size)
-        attn_w = gather_end(gather_pair(gather_pair(attn_far, size, 2), size, 1))
-        down_block, mlp_far = lax.optimization_barrier((w_down.reshape(FF // size, D), mlp_far))
-        mlp_x = gather_pair(mlp_far, size, 2)
-        down_far = gather_far(down_block, size)
-        mlp_w = gather_end(gather_pair(mlp_x, size, 1))
-        down_w = gather_end(gather_pair(gather_pair(down_far, size, 2), size, 1))
-        after_first, after_second = (token(mlp_far),), (token(mlp_x), token(down_far))
     else:
         whole = [
             lax.all_gather(w, "dp", axis=0, tiled=True).reshape(D, -1)
             for w in (w_query, w_key, w_value, w_out, w_gate, w_up)
         ]
         attn_w = jnp.concatenate(whole[:4], axis=1)
-        mlp_w = jnp.concatenate(whole[4:], axis=1)
+        gate_w, up_w = whole[4:]
         down_w = lax.all_gather(w_down, "dp", axis=0, tiled=True).reshape(FF, D)
-        after_first, after_second = (), ()
     qkv_w, out_w = attn_w[:, :QKV], attn_w[:, QKV:]
-    gate_w, up_w = mlp_w[:, :FF], mlp_w[:, FF:]
 
     seqs = hidden_in.shape[0]
     tokens = seqs * SEQ
@@ -308,10 +300,19 @@
     qkv = dot(qkv_w, h1, 0, 1)
     start = start.reshape(seqs, 1, SEQ)
     half = seqs // 2
-    share0, o, q0, k0, v0 = attend_forward(qkv, cos, sin, start, 0, half, after_first, None)
+    share0, o, q0, k0, v0 = attend_forward(qkv, cos, sin, start, 0, half, (), None)
+    if by_rows:
+        mlp_far, down_block, o = lax.optimization_barrier((mlp_far, down_block, o))
+        mlp_x = gather_pair(mlp_far, size, 2)
+        down_far = gather_far(down_block, size)
     share1, o, q1, k1, v1 = attend_forward(
-        qkv, cos, sin, start, half, seqs - half, after_second, o
+        qkv, cos, sin, start, half, seqs - half, (), o
     )
+    if by_rows:
+        mlp_x, down_far, o = lax.optimization_barrier((mlp_x, down_far, o))
+        mlp_w = gather_end(gather_pair(mlp_x, size, 1))
+        gate_w, up_w = mlp_w[:, :FF], mlp_w[:, FF:]
+        down_w = gather_end(gather_pair(gather_pair(down_far, size, 2), size, 1))
     m = x + dot(o, out_w, 0, 0)
     r2 = lax.rsqrt(jnp.mean(m * m, axis=-1, keepdims=True) + EPS)
     h2 = (m * r2 * gain_second).astype(BF16)
@@ -323,20 +324,11 @@
 
     gy = cotangent.reshape(tokens, D)
     d_down = dot(c, gy, 0, 0)
-    if by_rows:
-        d_down, gy = lax.optimization_barrier((d_down.astype(BF16), gy))
-        down_core = scatter_pair(scatter_begin(d_down, size), size, 1, 2)
     dc = dot(gy, down_w, 1, 1)
     da = (dc * b * s * (1.0 + a * (1.0 - s))).astype(BF16)
     db = (dc * a * s).astype(BF16)
     d_gate = dot(h2, da, 0, 0)
     d_up = dot(h2, db, 0, 0)
-    after_first, after_second = (), ()
-    if by_rows:
-        d_gu = jnp.concatenate([d_gate.astype(BF16), d_up.astype(BF16)], axis=1)
-        d_gu, down_core, da, db = lax.optimization_barrier((d_gu, down_core, da, db))
-        gu_core = scatter_pair(scatter_begin(d_gu, size), size, 1, 2)
-        down_x = scatter_pair(down_core, size, 2, 1)
     dh2 = dot(da, gate_w, 1, 1) + dot(db, up_w, 1, 1)
     g2 = jnp.sum(dh2 * m * r2, axis=0)
     e = dh2 * gain_second
@@ -344,14 +336,25 @@
     dmb = dm.astype(BF16)
     d_out = dot(o, dmb, 1, 0)
     do = dot(out_w, dmb, 1, 1).astype(BF16)
-    if by_rows:
+    after_first, after_second = (), ()
+    if by_rows:
+        d_gu = jnp.concatenate([d_gate.astype(BF16), d_up.astype(BF16)], axis=1)
+        d_down, d_gu, d_out, do = lax.optimization_barrier(
+            (d_down.astype(BF16), d_gu, d_out.astype(BF16), do)
+        )
+        down_core = scatter_pair(scatter_begin(d_down, size), size, 1, 2)
+        gu_core = scatter_pair(scatter_begin(d_gu, size), size, 1, 2)
+        after_first = (token(gu_core), token(down_core))
+    dqkv = attend_backward(share0, o, do, q0, k0, v0, cos, sin, 0, after_first, None)
+    if by_rows:
+        down_x = scatter_pair(down_core, size, 2, 1)
         gu_x = scatter_pair(gu_core, size, 2, 1)
+        d_out, down_x, dqkv = lax.optimization_barrier((d_out, down_x, dqkv))
+        out_core = scatter_pair(scatter_begin(d_out, size), size, 1, 2)
+    dqkv = attend_backward(share1, o, do, q1, k1, v1, cos, sin, half, after_second, dqkv)
+    if by_rows:
+        gu_x, out_core, dqkv = lax.optimization_barrier((gu_x, out_core, dqkv))
         down_z = scatter_far(down_x, size)
-        out_core = scatter_pair(scatter_begin(d_out, size), size, 1, 2)
-        after_first = (token(gu_core), token(down_x))
-        after_second = (token(gu_x), token(out_core), token(down_z))
-    dqkv = attend_backward(share0, o, do, q0, k0, v0, cos, sin, 0, after_first, None)
-    dqkv = attend_backward(share1, o, do, q1, k1, v1, cos, sin, half, after_second, dqkv)
     d_qkv = dot(h1, dqkv, 0, 1)
     dh1 = dot(dqkv, qkv_w, 0, 1)
     g1 = jnp.sum(dh1 * x * r1, axis=0)

time: 436 us -> 398 us (0.913); the launches traced: 428 us -> 400 us
  waiting for transfers between devices: 94 us -> 47.9 us
  Pallas kernels: 54.2 us -> 65 us
  starting transfers between devices: 49.5 us -> 57.3 us
  matrix products: 116 us -> 111 us
  local copies, waits for them, and re-layouts: 71.2 us -> 75.6 us
    ppermute x44, waiting for transfers between devices: 94 us -> 47.9 us  [swap(): return lax.ppermute(x, axis, [(i, i ^ bit) for i in range(size)])]
    pallas_call x2, Pallas kernels: 26.7 us -> 37.7 us  [attend_forward(): pl.pallas_call(attend_kernel, grid=(seqs,), in_specs=[col(QKV), col(HEAD_...]
    ppermute x44, starting transfers between devices: 49.5 us -> 57.3 us  [swap(): return lax.ppermute(x, axis, [(i, i ^ bit) for i in range(size)])]
    unnamed x136 -> x116, local copies, waits for them, and re-layouts: 8.85 us -> 15.7 us
    dot_general x15, matrix products: 116 us -> 111 us  [dot(): lax.dot_general(a, b, (((ca,), (cb,)), ((), ())), preferred_element_type=...]
    squeeze x8 -> x9, local copies, waits for them, and re-layouts: 9.22 us -> 7.84 us  [scatter_pair(): send = lax.dynamic_index_in_dim(held, 1 - side, axis, keepdims=False)]
  transfers between devices with their start and end apart: 44 -> 44, of which waited for: 21 -> 14; matrix products, arithmetic and copies ran while one was open for 23% -> 22% of each run, Pallas kernels for 9% -> 13%
where the time goes in v1:
time: 398 us; the launch traced here: 400 us
  matrix products  111 us (28%)
  local copies, waits for them, and re-layouts  75.6 us (19%)
  Pallas kernels  65 us (16%)
  starting transfers between devices  57.3 us (14%)
  waiting for transfers between devices  47.9 us (12%)
  other arithmetic  41.3 us (10%)
    dot_general x15, matrix products, dot(): lax.dot_general(a, b, (((ca,), (cb,)), ((), ())), preferred_element_type=...  111 us
    ppermute x44, starting transfers between devices, swap(): return lax.ppermute(x, axis, [(i, i ^ bit) for i in range(size)])  57.3 us
    ppermute x44, waiting for transfers between devices, swap(): return lax.ppermute(x, axis, [(i, i ^ bit) for i in range(size)])  47.9 us
    pallas_call x2, Pallas kernels, attend_forward(): pl.pallas_call(attend_kernel, grid=(seqs,), in_specs=[col(QKV), col(HEAD_...  37.7 us
    pallas_call x2, Pallas kernels, attend_backward(): pl.pallas_call(attend_back_kernel, grid=(seqs,), in_specs=[pl.BlockSpec((...  27.2 us
    unnamed x116, local copies, waits for them, and re-layouts  15.7 us
    reshape x3, local copies, waits for them, and re-layouts, scatter_begin(): return whole.astype(BF16).reshape(size // 4, 2, 2, rows, whole.shape[1])  8.27 us
  transfers between devices with their start and end apart: 44, of which 14 were waited for; matrix products, arithmetic and copies ran while one was open for 22% of the time, Pallas kernels for 13%

profile of v1, /device:TPU:0, one launch (start us, length us, event | category | flops | bytes accessed | tf_op | source)
XLA Modules:
  0.0 400.3 jit_solution(10298995491306043206)
XLA Ops:
  4.3 5.1 %collective-permute-start = (bf16[36,1536]{1,0:T(8,128)(2,1)S(1)}, bf16[36,1536]{1,0:T(8,128)(2,1)S(1)}, u32[]{:S(2)}, u32[]{:S(2)}) collective-permute-start(bf16[36,1536]{1,0:T(8,128)(2,1)S(1)} %concatenate.16), channel_id=1, source_target_pairs={{0,24},{2,26},{4,28},{6,30},{8,16},{10,18},{12,20},{14,22},{16,8},... | collective-permute-start | bytes 331784 | tf_op jit(solution)/shard_map/ppermute | solution.py:178
  10.1 4.5 %convert_bitcast_fusion = f32[4,72,8,512]{3,2,1,0:T(8,128)} fusion(bf16[4,512,576]{1,2,0:T(8,128)(2,1)} %param.12), kind=kLoop, calls=%fused_computation.10 | loop fusion | flops 1179648 | bytes 7077888
  15.6 5.3 %copy.125 = f32[4,72,8,512]{3,2,0,1:T(8,128)} copy(f32[4,72,8,512]{3,2,1,0:T(8,128)} %convert_bitcast_fusion) | data formatting | bytes 9437184 | tf_op jit(solution)/shard_map/convert_element_type | solution.py:297
  21.2 1.7 collective-permute-start.3
  24.1 9.6 %collective-permute-done.3 = bf16[4,36,1536]{2,1,0:T(8,128)(2,1)S(1)} collective-permute-done((bf16[4,36,1536]{2,1,0:T(8,128)(2,1)S(1)}, bf16[4,36,1536]{2,1,0:T(8,128)(2,1)S(1)}, u32[]{:S(2)}, u32[]{:S(2)}) %collective-permute-start.3) | collective-permute-done | bytes 442400 | tf_op jit(solution)/shard_map/ppermute | solution.py:178
  39.0 3.5 collective-permute-start.5
  43.4 9.3 %fusion.21.qkv_ref = f32[960,2048]{1,0:T(8,128)} fusion(bf16[576,1536]{1,0:T(8,128)(2,1)} %reshape.195, f32[2048,576]{0,1:T(8,128)} %bitcast.193, f32[576]{0:T(1024)S(1)} %convert_element_type.280, f32[2048]{0:T(1024)S(1)} %bitcast.218), kind=kOutput, calls=%fused_computation.60 | convolution fusion | flops 2268463104 | bytes 13773056 | tf_op jit(solution)/shard_map/dot_general | solution.py:33
  52.7 24.9 %attend_forward.2 = (bf16[2,9,768,256]{3,2,1,0:T(8,128)(2,1)S(1)}, bf16[576,2048]{1,0:T(8,128)(2,1)S(1)}, bf16[576,1024]{1,0:T(8,128)(2,1)S(1)}, bf16[192,1024]{1,0:T(8,128)(2,1)S(1)}, bf16[192,1024]{1,0:T(8,128)(2,1)S(1)}) custom-call(f32[960,2048]{1,0:T(8,128)} %fusion.21.qkv_ref, f32[64,2048]{1,0:T(8,128)S(1)} %get-tuple-element.179.cos_ref, ...), custom_call_target="tpu_custom_call" | custom-call | flops 10000000000 | bytes 16000000 | tf_op jit(solution)/shard_map/attend_forward/pallas_call | solution.py:76
  77.6 2.8 copy-done.7
  81.9 2.1 collective-permute-start.10
  84.0 2.0 collective-permute-start.11
  88.6 12.8 %attend_forward.3 = (bf16[2,9,768,256]{3,2,1,0:T(8,128)(2,1)S(1)}, bf16[576,2048]{1,0:T(8,128)(2,1)S(1)}, bf16[576,1024]{1,0:T(8,128)(2,1)S(1)}, bf16[192,1024]{1,0:T(8,128)(2,1)S(1)}, bf16[192,1024]{1,0:T(8,128)(2,1)S(1)}) custom-call(f32[960,2048]{1,0:T(8,128)} %fusion.21.qkv_ref, ...), custom_call_target="tpu_custom_call", output_to_operand_aliasing={{1}: (4, {})} | custom-call | flops 10000000000 | bytes 16000000 | tf_op jit(solution)/shard_map/attend_forward/pallas_call | solution.py:76
  102.7 4.4 %collective-permute-done.8 = bf16[4,36,3072]{2,0,1:T(4,128)(2,1)S(1)} collective-permute-done((bf16[4,36,3072]{2,0,1:T(4,128)(2,1)S(1)}, bf16[4,36,3072]{2,0,1:T(4,128)(2,1)S(1)}, u32[]{:S(2)}, u32[]{:S(2)}) %collective-permute-start.8) | collective-permute-done | bytes 884768 | tf_op jit(solution)/shard_map/ppermute | solution.py:178
  110.8 3.4 copy.126
  114.2 2.9 copy.99
  117.2 3.1 collective-permute-done.13
  121.8 5.0 %multiply_reduce_fusion.4 = (f32[2048]{0:T(1024)S(1)}, f32[2048,576]{0,1:T(8,128)S(1)}) fusion(f32[2048,576]{0,1:T(8,128)} %bitcast.194, bf16[576,2048]{1,0:T(8,128)(2,1)S(1)} %get-tuple-element.48.o_ref, bf16[576,1536]{1,0:T(8,128)(2,1)} %reshape.195), kind=kOutput, calls=%fused_computation.20 | convolution fusion | flops 1362491392 | bytes 12541952 | tf_op jit(solution)/shard_map/dot_general | solution.py:33
  126.8 2.2 multiply_convert_fusion.1
  132.9 2.2 copy.102
  135.1 4.7 %reshape.197 = bf16[576,3072]{1,0:T(8,128)(2,1)} reshape(bf16[4,2,2,36,3072]{4,3,2,1,0:T(8,128)(2,1)} %copy.102) | data formatting | bytes 7077888 | tf_op jit(solution)/shard_map/reshape | solution.py:205
  139.8 10.2 %fusion.10 = f32[2048,1536]{1,0:T(8,128)} fusion(bf16[2048,576]{0,1:T(8,128)(2,1)} %multiply_convert_fusion.1, bf16[576,3072]{1,0:T(8,128)(2,1)} %reshape.197), kind=kOutput, calls=%fused_computation.46 | convolution fusion | flops 3623878656 | bytes 16711680 | tf_op jit(solution)/shard_map/dot_general | solution.py:33
  149.9 8.5 %fusion.14 = f32[2048,1536]{1,0:T(8,128)} fusion(bf16[2048,576]{0,1:T(8,128)(2,1)S(1)} %copy-done.32, bf16[576,3072]{1,0:T(8,128)(2,1)S(1)} %copy-done.30), kind=kOutput, calls=%fused_computation.50 | convolution fusion | flops 3623878656 | bytes 16711680 | tf_op jit(solution)/shard_map/dot_general | solution.py:33
  158.4 21.3 %fusion.4 = (bf16[2048,1536]{1,0:T(8,128)(2,1)}, bf16[2048,1536]{1,0:T(8,128)(2,1)}, bf16[2048,1536]{1,0:T(8,128)(2,1)}) fusion(f32[2048,1536]{1,0:T(8,128)} %fusion.14, f32[2048,1536]{1,0:T(8,128)} %fusion.10, bf16[1536,576]{1,0:T(8,128)(2,1)} %bitcast.216, bf16[2048,576]{0,1:T(8,128)(2,1)} %bitcast.204), kind=kOutput, calls=%fused_computation.6 | convolution fusion | flops 3674210304 | bytes 48168960 | tf_op jit(solution)/shard_map/dot_general | solution.py:33
  179.7 9.5 %fusion.12 = f32[2048,576]{0,1:T(8,128)} fusion(bf16[2048,1536]{1,0:T(8,128)(2,1)} %get-tuple-element.131, bf16[576,3072]{1,0:T(8,128)(2,1)} %reshape.197), kind=kOutput, calls=%fused_computation.48 | convolution fusion | flops 3623878656 | bytes 12779520 | tf_op jit(solution)/shard_map/dot_general | solution.py:33
  189.2 7.6 %multiply_reduce_fusion = (f32[576]{0:T(1024)S(1)}, f32[2048]{0:T(1024)S(1)}, f32[2048,576]{0,1:T(8,128)S(1)}) fusion(f32[2048,576]{0,1:T(8,128)} %copy-done.20, f32[2048]{0:T(1024)S(1)} %add_rsqrt_fusion, f32[576]{0:T(1024)S(1)} %convert_element_type.285, f32[2048,576]{0,1:T(8,128)} %fusion.12, bf16[2048,1536]{1,0:T(8,128)(2,1)S(1)} %copy-done.46, ...), kind=kOutput, calls=%fused_computation.12 | convolution fusion | flops 3632133632 | bytes 22239488 | tf_op jit(solution)/shard_map/dot_general | solution.py:33
  196.9 1.9 multiply_add_fusion
  198.8 3.5 convolution_convert_fusion.1.do_ref
  202.2 2.9 convolution_convert_fusion.5
  205.2 6.8 %convolution_convert_fusion.3 = bf16[576,1536]{1,0:T(8,128)(2,1)S(1)} fusion(bf16[2048,576]{0,1:T(8,128)(2,1)S(1)} %copy-done.33, bf16[2048,1536]{1,0:T(8,128)(2,1)} %get-tuple-element.131), kind=kOutput, calls=%fused_computation.32 | convolution fusion | flops 3624763392 | bytes 10420224 | tf_op jit(solution)/shard_map/dot_general | solution.py:33
  212.0 3.8 convolution_convert_fusion.2
  215.9 5.2 %convolution_convert_fusion = bf16[1536,576]{0,1:T(8,128)(2,1)} fusion(bf16[2048,576]{0,1:T(8,128)(2,1)S(1)} %bitcast.206, bf16[2048,1536]{1,0:T(8,128)(2,1)S(1)} %bitcast.226), kind=kOutput, calls=%fused_computation.29 | convolution fusion | flops 3624763392 | bytes 10420224 | tf_op jit(solution)/shard_map/dot_general | solution.py:33
  221.0 2.3 pad_maximum_fusion
  223.3 3.9 copy.112
  227.2 2.2 dynamic-slice_bitcast_fusion.1
  229.9 4.7 %reshape.201 = bf16[4,2,2,36,3072]{4,3,2,1,0:T(8,128)(2,1)} reshape(bf16[576,3072]{1,0:T(8,128)(2,1)} %pad_maximum_fusion) | data formatting | bytes 7077888 | tf_op jit(solution)/shard_map/reshape | solution.py:210
  234.6 1.8 dynamic-slice_bitcast_fusion
  241.0 6.8 %add_convert_fusion.1 = bf16[2048,576]{0,1:T(8,128)(2,1)S(1)} fusion(f32[2048,576]{0,1:T(8,128)S(1)} %bitcast.203, bf16[2048,1536]{1,0:T(8,128)(2,1)} %get-tuple-element.132, bf16[1536,576]{1,0:T(8,128)(2,1)S(1)} %bitcast.217), kind=kOutput, calls=%fused_computation.18 | convolution fusion | flops 3626237952 | bytes 15138816 | tf_op jit(solution)/shard_map/dot_general | solution.py:33
  247.9 1.6 copy.142
  249.5 3.6 collective-permute-done.18
  256.7 13.7 %attend_backward.2.refs_0_ = bf16[960,2048]{1,0:T(8,128)(2,1)S(1)} custom-call(bf16[2,9,768,256]{3,2,1,0:T(8,128)(2,1)} %copy-done.7, bf16[576,2048]{1,0:T(8,128)(2,1)S(1)} %get-tuple-element.48.o_ref, bf16[576,2048]{1,0:T(8,128)(2,1)S(1)} %copy-done.4, bf16[576,1024]{1,0:T(8,128)(2,1)S(1)} %copy-done.11, bf16[192,1024]{1,0:T(8,128)(2,1)S(1)} %copy-done.17, ...), custom_call_target="tpu_custom_call" | custom-call | flops 20000000000 | bytes 16000000 | tf_op jit(solution)/shard_map/attend_backward/pallas_call | solution.py:152
  270.4 1.9 copy-done
  274.0 3.2 collective-permute-start.41
  277.5 2.2 reshape.205
  279.7 1.8 dynamic-slice_bitcast_fusion.4
  281.5 2.8 copy.143
  289.7 2.1 copy-done.1
  291.8 1.7 copy-done.5
  296.7 13.5 %attend_backward.3 = bf16[960,2048]{1,0:T(8,128)(2,1)S(1)} custom-call(bf16[2,9,768,256]{3,2,1,0:T(8,128)(2,1)} %copy-done.6, bf16[576,2048]{1,0:T(8,128)(2,1)S(1)} %get-tuple-element.48.o_ref, bf16[576,2048]{1,0:T(8,128)(2,1)S(1)} %copy-done.5, bf16[576,1024]{1,0:T(8,128)(2,1)S(1)} %copy-done.9, ...), custom_call_target="tpu_custom_call", output_to_operand_aliasing={{}: (8, {})} | custom-call | flops 20000000000 | bytes 16000000 | tf_op jit(solution)/shard_map/attend_backward/pallas_call | solution.py:152
  310.2 1.9 copy-done.2
  314.4 1.9 fusion.8
  316.4 6.2 %convolution_convert_fusion.4 = bf16[576,960]{1,0:T(8,128)(2,1)} fusion(bf16[960,2048]{1,0:T(8,128)(2,1)S(1)} %copy-done.3, f32[2048,576]{0,1:T(8,128)} %bitcast.195, f32[576]{0:T(1024)S(1)} %copy-done.43, f32[2048]{0:T(1024)S(1)} %bitcast.219), kind=kOutput, calls=%fused_computation.52 | convolution fusion | flops 2269016064 | bytes 9767168 | tf_op jit(solution)/shard_map/dot_general | solution.py:33
  322.6 4.7 %multiply_reduce_fusion.1 = (f32[576]{0:T(1024)S(1)}, f32[2048]{0:T(1024)S(1)}, f32[2048,576]{0,1:T(8,128)}) fusion(f32[2048,576]{0,1:T(8,128)S(1)} %bitcast.199, f32[2048]{0:T(1024)S(1)} %bitcast.220, f32[576]{0:T(1024)S(1)} %copy-done.43, bf16[960,2048]{1,0:T(8,128)(2,1)S(1)} %copy-done.3, bf16[576,1536]{1,0:T(8,128)(2,1)S(1)} %copy-done.29), kind=kOutput, calls=%fused_computation.13 | convolution fusion | flops 2271999488 | bytes 14571776 | tf_op jit(solution)/shard_map/dot_general | solution.py:33
  328.2 1.9 collective-permute-start.36
  334.9 2.6 collective-permute-done.22
  337.5 2.2 collective-permute-start.23
  339.7 2.3 collective-permute-done.23
  342.6 7.0 %add_convert_fusion = bf16[2048,576]{0,1:T(8,128)(2,1)S(1)} fusion(f32[2048,576]{0,1:T(8,128)} %copy-done.21, f32[2048,576]{0,1:T(8,128)} %get-tuple-element.178, f32[2048,576]{0,1:T(8,128)} %bitcast.196, f32[2048]{0:T(1024)S(1)} %broadcast_multiply_fusion, f32[576]{0:T(1024)S(1)} %copy-done.43, f32[2048]{0:T(1024)S(1)} %bitcast.221), kind=kLoop, calls=%fused_computation.14 | loop fusion | flops 9437184 | bytes 16533760 | tf_op jit(solution)/shard_map/convert_element_type | solution.py:363
  353.6 1.6 collective-permute-start.33
  358.7 9.4 %collective-permute-done.33 = bf16[36,576]{1,0:T(8,128)(2,1)S(1)} collective-permute-done((bf16[36,576]{1,0:T(8,128)(2,1)S(1)}, bf16[36,576]{1,0:T(8,128)(2,1)S(1)}, u32[]{:S(2)}, u32[]{:S(2)}) %collective-permute-start.33) | collective-permute-done | bytes 41504 | tf_op jit(solution)/shard_map/ppermute | solution.py:178
  368.1 2.4 collective-permute-start.38
  374.0 3.1 collective-permute-done.37
  380.7 4.7 %collective-permute-start.27 = (bf16[36,960]{1,0:T(8,128)(2,1)S(1)}, bf16[36,960]{1,0:T(8,128)(2,1)S(1)}, u32[]{:S(2)}, u32[]{:S(2)}) collective-permute-start(bf16[36,960]{1,0:T(8,128)(2,1)S(1)} %get-tuple-element.165), channel_id=1, source_target_pairs={{0,8},{2,10},{4,12},{6,14},{8,0},{10,2},{12,4},{14,6},{16,24},{18,... | collective-permute-start | bytes 207368 | tf_op jit(solution)/shard_map/ppermute | solution.py:178
  388.5 4.9 %collective-permute-done.28 = bf16[36,960]{1,0:T(8,128)(2,1)S(1)} collective-permute-done((bf16[36,960]{1,0:T(8,128)(2,1)S(1)}, bf16[36,960]{1,0:T(8,128)(2,1)S(1)}, u32[]{:S(2)}, u32[]{:S(2)}) %collective-permute-start.28) | collective-permute-done | bytes 69152 | tf_op jit(solution)/shard_map/ppermute | solution.py:178
  395.4 2.5 collective-permute-done.30
  (276 shorter events, 76.6 us)
Async XLA Ops:
  0.6 14.0 %copy-start.24 = (bf16[4,512,576]{1,2,0:T(8,128)(2,1)S(1)}, bf16[4,512,576]{1,2,0:T(8,128)(2,1)}, u32[]{:S(2)}) copy-start(bf16[4,512,576]{1,2,0:T(8,128)(2,1)} %param.12) | copy-start | bytes 7077892
  4.3 10.8 %copy-start.36 = (bf16[55296]{0:T(1024)(128)(2,1)S(1)}, bf16[55296]{0:T(1024)(128)(2,1)}, u32[]{:S(2)}) copy-start(bf16[55296]{0:T(1024)(128)(2,1)} %param.20) | copy-start | bytes 331780
  4.3 11.0 %copy-start.37 = (bf16[55296]{0:T(1024)(128)(2,1)S(1)}, bf16[55296]{0:T(1024)(128)(2,1)}, u32[]{:S(2)}) copy-start(bf16[55296]{0:T(1024)(128)(2,1)} %param.21) | copy-start | bytes 331780
  4.3 11.1 %copy-start.38 = (bf16[55296]{0:T(1024)(128)(2,1)S(1)}, bf16[55296]{0:T(1024)(128)(2,1)}, u32[]{:S(2)}) copy-start(bf16[55296]{0:T(1024)(128)(2,1)} %param.22) | copy-start | bytes 331780
  4.3 16.7 %collective-permute-start = (bf16[36,1536]{1,0:T(8,128)(2,1)S(1)}, bf16[36,1536]{1,0:T(8,128)(2,1)S(1)}, u32[]{:S(2)}, u32[]{:S(2)}) collective-permute-start(bf16[36,1536]{1,0:T(8,128)(2,1)S(1)} %concatenate.16), channel_id=1, source_target_pairs={{0,24},{2,26},{4,28},{6,30},{8,16},{10,18},{12,20},{14,22},{16,8},... | collective-permute-start | bytes 331784 | tf_op jit(solution)/shard_map/ppermute | solution.py:178
  9.5 11.6 %collective-permute-start.1 = (bf16[36,1536]{1,0:T(8,128)(2,1)S(1)}, bf16[36,1536]{1,0:T(8,128)(2,1)S(1)}, u32[]{:S(2)}, u32[]{:S(2)}) collective-permute-start(bf16[36,1536]{1,0:T(8,128)(2,1)S(1)} %concatenate.16), channel_id=1, source_target_pairs={{0,16},{2,18},{4,20},{6,22},{8,24},{10,26},{12,28},{14,30},{16,0},... | collective-permute-start | bytes 331784 | tf_op jit(solution)/shard_map/ppermute | solution.py:178
  9.5 11.6 %collective-permute-start.2 = (bf16[36,1536]{1,0:T(8,128)(2,1)S(1)}, bf16[36,1536]{1,0:T(8,128)(2,1)S(1)}, u32[]{:S(2)}, u32[]{:S(2)}) collective-permute-start(bf16[36,1536]{1,0:T(8,128)(2,1)S(1)} %concatenate.16), channel_id=1, source_target_pairs={{0,8},{2,10},{4,12},{6,14},{8,0},{10,2},{12,4},{14,6},{16,24},{18,... | collective-permute-start | bytes 331784 | tf_op jit(solution)/shard_map/ppermute | solution.py:178
  21.0 22.4 %copy-start.39 = (f32[1,4,4,128]{3,1,2,0:T(4,128)}, f32[1,4,4,128]{3,1,2,0:T(4,128)S(1)}, u32[]{:S(2)}) copy-start(f32[1,4,4,128]{3,1,2,0:T(4,128)S(1)} %copy.127) | copy-start | bytes 24580
  21.0 22.4 %copy-start.42 = (f32[576]{0:T(1024)}, f32[576]{0:T(1024)S(1)}, u32[]{:S(2)}) copy-start(f32[576]{0:T(1024)S(1)} %convert_element_type.280) | copy-start | bytes 6916
  21.2 12.5 %collective-permute-start.3 = (bf16[4,36,1536]{2,1,0:T(8,128)(2,1)S(1)}, bf16[4,36,1536]{2,1,0:T(8,128)(2,1)S(1)}, u32[]{:S(2)}, u32[]{:S(2)}) collective-permute-start(bf16[4,36,1536]{2,1,0:T(8,128)(2,1)S(1)} %pad_maximum_fusion.8), channel_id=1, source_target_pairs={{0,4},{2,6},{4,0},{6,2},{8,12},{10,14},{12,8},{14,10},{16,20},{18,... | collective-permute-start | bytes 1327112 | tf_op jit(solution)/shard_map/ppermute | solution.py:178
  34.3 2.5 collective-permute-start.4
  39.0 41.4 %collective-permute-start.5 = (bf16[36,3072]{1,0:T(8,128)(2,1)}, bf16[36,3072]{1,0:T(8,128)(2,1)S(1)}, u32[]{:S(2)}, u32[]{:S(2)}) collective-permute-start(bf16[36,3072]{1,0:T(8,128)(2,1)} %pad_maximum_fusion.10), channel_id=1, source_target_pairs={{0,24},{2,26},{4,28},{6,30},{8,16},{10,18},{12,20},{14,22},{16,8},... | collective-permute-start | bytes 663560 | tf_op jit(solution)/shard_map/ppermute | solution.py:178
  42.5 38.0 %collective-permute-start.6 = (bf16[36,3072]{1,0:T(8,128)(2,1)}, bf16[36,3072]{1,0:T(8,128)(2,1)S(1)}, u32[]{:S(2)}, u32[]{:S(2)}) collective-permute-start(bf16[36,3072]{1,0:T(8,128)(2,1)} %pad_maximum_fusion.10), channel_id=1, source_target_pairs={{0,16},{2,18},{4,20},{6,22},{8,24},{10,26},{12,28},{14,30},{16,0},... | collective-permute-start | bytes 663560 | tf_op jit(solution)/shard_map/ppermute | solution.py:178
  42.5 38.0 %collective-permute-start.7 = (bf16[36,3072]{1,0:T(8,128)(2,1)}, bf16[36,3072]{1,0:T(8,128)(2,1)S(1)}, u32[]{:S(2)}, u32[]{:S(2)}) collective-permute-start(bf16[36,3072]{1,0:T(8,128)(2,1)} %pad_maximum_fusion.10), channel_id=1, source_target_pairs={{0,8},{2,10},{4,12},{6,14},{8,0},{10,2},{12,4},{14,6},{16,24},{18,... | collective-permute-start | bytes 663560 | tf_op jit(solution)/shard_map/ppermute | solution.py:178
  81.9 19.6 %collective-permute-start.10 = (bf16[96,576]{1,0:T(8,128)(2,1)S(1)}, bf16[96,576]{1,0:T(8,128)(2,1)S(1)}, u32[]{:S(2)}, u32[]{:S(2)}) collective-permute-start(bf16[96,576]{1,0:T(8,128)(2,1)S(1)} %reshape.190), channel_id=1, source_target_pairs={{0,16},{2,18},{4,20},{6,22},{8,24},{10,26},{12,28},{14,30},{16,0},... | collective-permute-start | bytes 331784 | tf_op jit(solution)/shard_map/ppermute | solution.py:178
  84.0 17.6 %collective-permute-start.11 = (bf16[96,576]{1,0:T(8,128)(2,1)S(1)}, bf16[96,576]{1,0:T(8,128)(2,1)S(1)}, u32[]{:S(2)}, u32[]{:S(2)}) collective-permute-start(bf16[96,576]{1,0:T(8,128)(2,1)S(1)} %reshape.190), channel_id=1, source_target_pairs={{0,8},{2,10},{4,12},{6,14},{8,0},{10,2},{12,4},{14,6},{16,24},{18,... | collective-permute-start | bytes 331784 | tf_op jit(solution)/shard_map/ppermute | solution.py:178
  86.0 15.5 %collective-permute-start.9 = (bf16[96,576]{1,0:T(8,128)(2,1)S(1)}, bf16[96,576]{1,0:T(8,128)(2,1)S(1)}, u32[]{:S(2)}, u32[]{:S(2)}) collective-permute-start(bf16[96,576]{1,0:T(8,128)(2,1)S(1)} %reshape.190), channel_id=1, source_target_pairs={{0,24},{2,26},{4,28},{6,30},{8,16},{10,18},{12,20},{14,22},{16,8},... | collective-permute-start | bytes 331784 | tf_op jit(solution)/shard_map/ppermute | solution.py:178
  87.1 20.1 %collective-permute-start.8 = (bf16[4,36,3072]{2,0,1:T(4,128)(2,1)S(1)}, bf16[4,36,3072]{2,0,1:T(4,128)(2,1)S(1)}, u32[]{:S(2)}, u32[]{:S(2)}) collective-permute-start(bf16[4,36,3072]{2,0,1:T(4,128)(2,1)S(1)} %copy.96), channel_id=1, source_target_pairs={{0,4},{2,6},{4,0},{6,2},{8,12},{10,14},{12,8},{14,10},{16,20},{18,... | collective-permute-start | bytes 2654216 | tf_op jit(solution)/shard_map/ppermute | solution.py:178
  101.5 7.7 %copy-start.6 = (bf16[2,9,768,256]{3,2,1,0:T(8,128)(2,1)}, bf16[2,9,768,256]{3,2,1,0:T(8,128)(2,1)S(1)}, u32[]{:S(2)}) copy-start(bf16[2,9,768,256]{3,2,1,0:T(8,128)(2,1)S(1)} %get-tuple-element.60.p_ref) | copy-start | bytes 21233668
  101.5 7.7 %copy-start.8 = (bf16[576,1024]{1,0:T(8,128)(2,1)}, bf16[576,1024]{1,0:T(8,128)(2,1)S(1)}, u32[]{:S(2)}) copy-start(bf16[576,1024]{1,0:T(8,128)(2,1)S(1)} %get-tuple-element.61.q_ref) | copy-start | bytes 3538948
  101.5 7.7 %copy-start.12 = (bf16[192,1024]{1,0:T(8,128)(2,1)}, bf16[192,1024]{1,0:T(8,128)(2,1)S(1)}, u32[]{:S(2)}) copy-start(bf16[192,1024]{1,0:T(8,128)(2,1)S(1)} %get-tuple-element.62.k_ref) | copy-start | bytes 1179652
  101.5 7.7 %copy-start.14 = (bf16[192,1024]{1,0:T(8,128)(2,1)}, bf16[192,1024]{1,0:T(8,128)(2,1)S(1)}, u32[]{:S(2)}) copy-start(bf16[192,1024]{1,0:T(8,128)(2,1)S(1)} %get-tuple-element.63.v_ref) | copy-start | bytes 1179652
  102.7 8.0 %copy-start.45 = (bf16[576]{0:T(1024)(128)(2,1)S(1)}, bf16[576]{0:T(1024)(128)(2,1)}, u32[]{:S(2)}) copy-start(bf16[576]{0:T(1024)(128)(2,1)} %param.19) | copy-start | bytes 3460
  109.2 11.0 %collective-permute-start.13 = (bf16[4,96,576]{2,1,0:T(8,128)(2,1)}, bf16[4,96,576]{2,1,0:T(8,128)(2,1)}, u32[]{:S(2)}, u32[]{:S(2)}) collective-permute-start(bf16[4,96,576]{2,1,0:T(8,128)(2,1)} %pad_maximum_fusion.9), channel_id=1, source_target_pairs={{0,4},{2,6},{4,0},{6,2},{8,12},{10,14},{12,8},{14,10},{16,20},{18,... | collective-permute-start | bytes 1327112 | tf_op jit(solution)/shard_map/ppermute | solution.py:178
  117.1 14.1 %collective-permute-start.12 = (bf16[2,4,36,3072]{3,1,2,0:T(4,128)(2,1)S(1)}, bf16[2,4,36,3072]{3,1,2,0:T(4,128)(2,1)S(1)}, u32[]{:S(2)}, u32[]{:S(2)}) collective-permute-start(bf16[2,4,36,3072]{3,1,2,0:T(4,128)(2,1)S(1)} %copy.99), channel_id=1, source_target_pairs={{0,2},{2,0},{4,6},{6,4},{8,10},{10,8},{12,14},{14,12},{16,18},{18,... | collective-permute-start | bytes 5308424 | tf_op jit(solution)/shard_map/ppermute | solution.py:178
  121.7 7.3 %collective-permute-start.14 = (bf16[2,4,96,576]{3,2,0,1:T(8,128)(2,1)S(1)}, bf16[2,4,96,576]{3,2,0,1:T(8,128)(2,1)S(1)}, u32[]{:S(2)}, u32[]{:S(2)}) collective-permute-start(bf16[2,4,96,576]{3,2,0,1:T(8,128)(2,1)S(1)} %pad_maximum_fusion.5), channel_id=1, source_target_pairs={{0,2},{2,0},{4,6},{6,4},{8,10},{10,8},{12,14},{14,12},{16,18},{18,... | collective-permute-start | bytes 2654216 | tf_op jit(solution)/shard_map/ppermute | solution.py:178
  139.7 10.2 %copy-start.30 = (bf16[576,3072]{1,0:T(8,128)(2,1)S(1)}, bf16[576,3072]{1,0:T(8,128)(2,1)}, u32[]{:S(2)}) copy-start(bf16[576,3072]{1,0:T(8,128)(2,1)} %reshape.197) | copy-start | bytes 10616836
  139.7 10.2 %copy-start.32 = (bf16[2048,576]{0,1:T(8,128)(2,1)S(1)}, bf16[2048,576]{0,1:T(8,128)(2,1)}, u32[]{:S(2)}) copy-start(bf16[2048,576]{0,1:T(8,128)(2,1)} %multiply_convert_fusion.1) | copy-start | bytes 7077892
  179.7 9.5 %copy-start.31 = (bf16[576,3072]{1,0:T(8,128)(2,1)S(1)}, bf16[576,3072]{1,0:T(8,128)(2,1)}, u32[]{:S(2)}) copy-start(bf16[576,3072]{1,0:T(8,128)(2,1)} %reshape.197) | copy-start | bytes 10616836
  179.7 9.5 %copy-start.46 = (bf16[2048,1536]{1,0:T(8,128)(2,1)S(1)}, bf16[2048,1536]{1,0:T(8,128)(2,1)}, u32[]{:S(2)}) copy-start(bf16[2048,1536]{1,0:T(8,128)(2,1)} %get-tuple-element.130) | copy-start | bytes 18874372
  179.7 17.1 %slice-start.2 = ((s8[4718592]{0:T(1024)(128)(4,1)}), s8[4194304]{0:T(1024)(128)(4,1)S(1)}, s32[]{:S(2)}) async-start(s8[4718592]{0:T(1024)(128)(4,1)} %bitcast.200), calls=%async_computation.2 | async-start | bytes 8388608
  202.2 9.7 %slice-start.6 = ((s8[6291456]{0:T(1024)(128)(4,1)}), s8[4194304]{0:T(1024)(128)(4,1)S(1)}, s32[]{:S(2)}) async-start(s8[6291456]{0:T(1024)(128)(4,1)} %bitcast.223), calls=%async_computation.6 | async-start | bytes 8388608
  205.2 10.7 %slice-start.8 = ((s8[6291456]{0:T(1024)(128)(4,1)}), s8[4194304]{0:T(1024)(128)(4,1)S(1)}, s32[]{:S(2)}) async-start(s8[6291456]{0:T(1024)(128)(4,1)} %bitcast.225), calls=%async_computation.8 | async-start | bytes 8388608
  229.4 8.5 %collective-permute-start.17 = (bf16[4,2,96,576]{3,2,1,0:T(8,128)(2,1)}, bf16[4,2,96,576]{3,2,1,0:T(8,128)(2,1)}, u32[]{:S(2)}, u32[]{:S(2)}) collective-permute-start(bf16[4,2,96,576]{3,2,1,0:T(8,128)(2,1)} %dynamic-slice_bitcast_fusion.1), channel_id=1, source_target_pairs={{0,2},{2,0},{4,6},{6,4},{8,10},{10,8},{12,14},{14,12},{16,18},{18,... | collective-permute-start | bytes 2654216 | tf_op jit(solution)/shard_map/ppermute | solution.py:178
  237.9 15.5 %collective-permute-start.15 = (bf16[4,2,36,3072]{3,0,2,1:T(4,128)(2,1)S(1)}, bf16[4,2,36,3072]{3,0,2,1:T(4,128)(2,1)S(1)}, u32[]{:S(2)}, u32[]{:S(2)}) collective-permute-start(bf16[4,2,36,3072]{3,0,2,1:T(4,128)(2,1)S(1)} %copy.108), channel_id=1, source_target_pairs={{0,2},{2,0},{4,6},{6,4},{8,10},{10,8},{12,14},{14,12},{16,18},{18,... | collective-permute-start | bytes 5308424 | tf_op jit(solution)/shard_map/ppermute | solution.py:178
  239.5 13.7 %collective-permute-start.18 = (bf16[4,96,576]{2,1,0:T(8,128)(2,1)S(1)}, bf16[4,96,576]{2,1,0:T(8,128)(2,1)S(1)}, u32[]{:S(2)}, u32[]{:S(2)}) collective-permute-start(bf16[4,96,576]{2,1,0:T(8,128)(2,1)S(1)} %dynamic-slice_bitcast_fusion.3), channel_id=1, source_target_pairs={{0,4},{2,6},{4,0},{6,2},{8,12},{10,14},{12,8},{14,10},{16,20},{18,... | collective-permute-start | bytes 1327112 | tf_op jit(solution)/shard_map/ppermute | solution.py:178
  253.3 17.2 %copy-start.35 = (bf16[4,96,576]{2,1,0:T(8,128)(2,1)}, bf16[4,96,576]{2,1,0:T(8,128)(2,1)S(1)}, u32[]{:S(2)}) copy-start(bf16[4,96,576]{2,1,0:T(8,128)(2,1)S(1)} %fusion.23) | copy-start | bytes 1327108
  273.1 12.7 %collective-permute-start.40 = (bf16[96,576]{1,0:T(8,128)(2,1)}, bf16[96,576]{1,0:T(8,128)(2,1)}, u32[]{:S(2)}, u32[]{:S(2)}) collective-permute-start(bf16[96,576]{1,0:T(8,128)(2,1)} %get-tuple-element.152), channel_id=1, source_target_pairs={{0,8},{2,10},{4,12},{6,14},{8,0},{10,2},{12,4},{14,6},{16,24},{18,... | collective-permute-start | bytes 331784 | tf_op jit(solution)/shard_map/ppermute | solution.py:178
  274.0 13.0 %collective-permute-start.41 = (bf16[96,576]{1,0:T(8,128)(2,1)}, bf16[96,576]{1,0:T(8,128)(2,1)}, u32[]{:S(2)}, u32[]{:S(2)}) collective-permute-start(bf16[96,576]{1,0:T(8,128)(2,1)} %get-tuple-element.154), channel_id=1, source_target_pairs={{0,16},{2,18},{4,20},{6,22},{8,24},{10,26},{12,28},{14,30},{16,0},... | collective-permute-start | bytes 331784 | tf_op jit(solution)/shard_map/ppermute | solution.py:178
  277.1 9.8 %collective-permute-start.42 = (bf16[96,576]{1,0:T(8,128)(2,1)S(1)}, bf16[96,576]{1,0:T(8,128)(2,1)}, u32[]{:S(2)}, u32[]{:S(2)}) collective-permute-start(bf16[96,576]{1,0:T(8,128)(2,1)S(1)} %get-tuple-element.153), channel_id=1, source_target_pairs={{0,24},{2,26},{4,28},{6,30},{8,16},{10,18},{12,20},{14,22},{16,8},... | collective-permute-start | bytes 331784 | tf_op jit(solution)/shard_map/ppermute | solution.py:178
  281.5 31.5 %collective-permute-start.19 = (bf16[4,2,36,576]{3,2,1,0:T(8,128)(2,1)}, bf16[4,2,36,576]{3,2,1,0:T(8,128)(2,1)}, u32[]{:S(2)}, u32[]{:S(2)}) collective-permute-start(bf16[4,2,36,576]{3,2,1,0:T(8,128)(2,1)} %dynamic-slice_bitcast_fusion.4), channel_id=1, source_target_pairs={{0,2},{2,0},{4,6},{6,4},{8,10},{10,8},{12,14},{14,12},{16,18},{18,... | collective-permute-start | bytes 995336 | tf_op jit(solution)/shard_map/ppermute | solution.py:178
  284.3 30.1 %collective-permute-start.16 = (bf16[4,36,3072]{2,0,1:T(4,128)(2,1)}, bf16[4,36,3072]{2,0,1:T(4,128)(2,1)}, u32[]{:S(2)}, u32[]{:S(2)}) collective-permute-start(bf16[4,36,3072]{2,0,1:T(4,128)(2,1)} %bitcast.192), channel_id=1, source_target_pairs={{0,4},{2,6},{4,0},{6,2},{8,12},{10,14},{12,8},{14,10},{16,20},{18,... | collective-permute-start | bytes 2654216 | tf_op jit(solution)/shard_map/ppermute | solution.py:178
  288.1 24.1 %collective-permute-start.43 = (bf16[96,576]{1,0:T(8,128)(2,1)S(1)}, bf16[96,576]{1,0:T(8,128)(2,1)S(1)}, u32[]{:S(2)}, u32[]{:S(2)}) collective-permute-start(bf16[96,576]{1,0:T(8,128)(2,1)S(1)} %fusion.34), channel_id=1, source_target_pairs={{0,1},{1,0},{2,3},{3,2},{4,5},{5,4},{6,7},{7,6},{8,9},{9,8},{10,11... | collective-permute-start | bytes 331784 | tf_op jit(solution)/shard_map/ppermute | solution.py:178
  312.2 10.4 %slice-start = ((s8[4718592]{0:T(1024)(128)(4,1)}), s8[524288]{0:T(1024)(128)(4,1)S(1)}, s32[]{:S(2)}) async-start(s8[4718592]{0:T(1024)(128)(4,1)} %bitcast.197), calls=%async_computation | async-start | bytes 1048576
  327.4 2.8 collective-permute-start.20
  328.2 45.8 %collective-permute-start.36 = (bf16[36,3072]{1,0:T(8,128)(2,1)}, bf16[36,3072]{1,0:T(8,128)(2,1)}, u32[]{:S(2)}, u32[]{:S(2)}) collective-permute-start(bf16[36,3072]{1,0:T(8,128)(2,1)} %get-tuple-element.141), channel_id=1, source_target_pairs={{0,8},{2,10},{4,12},{6,14},{8,0},{10,2},{12,4},{14,6},{16,24},{18,... | collective-permute-start | bytes 663560 | tf_op jit(solution)/shard_map/ppermute | solution.py:178
  330.1 3.7 collective-permute-start.21
  331.7 19.4 %collective-permute-start.31 = (bf16[4,36,576]{2,1,0:T(8,128)(2,1)S(1)}, bf16[4,36,576]{2,1,0:T(8,128)(2,1)}, u32[]{:S(2)}, u32[]{:S(2)}) collective-permute-start(bf16[4,36,576]{2,1,0:T(8,128)(2,1)S(1)} %dynamic-slice_bitcast_fusion.9), channel_id=1, source_target_pairs={{0,4},{2,6},{4,0},{6,2},{8,12},{10,14},{12,8},{14,10},{16,20},{18,... | collective-permute-start | bytes 497672 | tf_op jit(solution)/shard_map/ppermute | solution.py:178
  333.8 3.7 collective-permute-start.22
  334.8 37.3 %collective-permute-start.25 = (bf16[4,2,36,960]{3,0,2,1:T(4,128)(2,1)S(1)}, bf16[4,2,36,960]{3,0,2,1:T(4,128)(2,1)S(1)}, u32[]{:S(2)}, u32[]{:S(2)}) collective-permute-start(bf16[4,2,36,960]{3,0,2,1:T(4,128)(2,1)S(1)} %copy.114), channel_id=1, source_target_pairs={{0,2},{2,0},{4,6},{6,4},{8,10},{10,8},{12,14},{14,12},{16,18},{18,... | collective-permute-start | bytes 1658888 | tf_op jit(solution)/shard_map/ppermute | solution.py:178
  337.5 4.5 %collective-permute-start.23 = (f32[2,576]{1,0:T(2,128)S(1)}, f32[2,576]{1,0:T(2,128)S(1)}, u32[]{:S(2)}, u32[]{:S(2)}) collective-permute-start(f32[2,576]{1,0:T(2,128)S(1)} %add.208), channel_id=1, source_target_pairs={{0,16},{2,18},{4,20},{6,22},{8,24},{10,26},{12,28},{14,30},{16,0},... | collective-permute-start | bytes 13832 | tf_op jit(solution)/shard_map/ppermute | solution.py:178
  342.0 9.1 %collective-permute-start.24 = (f32[2,576]{1,0:T(2,128)S(1)}, f32[2,576]{1,0:T(2,128)S(1)}, u32[]{:S(2)}, u32[]{:S(2)}) collective-permute-start(f32[2,576]{1,0:T(2,128)S(1)} %add.209), channel_id=1, source_target_pairs={{0,1},{1,0},{2,3},{3,2},{4,5},{5,4},{6,7},{7,6},{8,9},{9,8},{10,11... | collective-permute-start | bytes 13832 | tf_op jit(solution)/shard_map/ppermute | solution.py:178
  352.2 5.1 %collective-permute-start.32 = (bf16[36,576]{1,0:T(8,128)(2,1)S(1)}, bf16[36,576]{1,0:T(8,128)(2,1)S(1)}, u32[]{:S(2)}, u32[]{:S(2)}) collective-permute-start(bf16[36,576]{1,0:T(8,128)(2,1)S(1)} %get-tuple-element.168), channel_id=1, source_target_pairs={{0,8},{2,10},{4,12},{6,14},{8,0},{10,2},{12,4},{14,6},{16,24},{18,... | collective-permute-start | bytes 124424 | tf_op jit(solution)/shard_map/ppermute | solution.py:178
  353.6 14.6 %collective-permute-start.33 = (bf16[36,576]{1,0:T(8,128)(2,1)S(1)}, bf16[36,576]{1,0:T(8,128)(2,1)S(1)}, u32[]{:S(2)}, u32[]{:S(2)}) collective-permute-start(bf16[36,576]{1,0:T(8,128)(2,1)S(1)} %get-tuple-element.170), channel_id=1, source_target_pairs={{0,16},{2,18},{4,20},{6,22},{8,24},{10,26},{12,28},{14,30},{16,0},... | collective-permute-start | bytes 124424 | tf_op jit(solution)/shard_map/ppermute | solution.py:178
  355.2 15.3 %collective-permute-start.34 = (bf16[36,576]{1,0:T(8,128)(2,1)S(1)}, bf16[36,576]{1,0:T(8,128)(2,1)S(1)}, u32[]{:S(2)}, u32[]{:S(2)}) collective-permute-start(bf16[36,576]{1,0:T(8,128)(2,1)S(1)} %get-tuple-element.169), channel_id=1, source_target_pairs={{0,24},{2,26},{4,28},{6,30},{8,16},{10,18},{12,20},{14,22},{16,8},... | collective-permute-start | bytes 124424 | tf_op jit(solution)/shard_map/ppermute | solution.py:178
  357.3 19.9 %collective-permute-start.37 = (bf16[36,3072]{1,0:T(8,128)(2,1)S(1)}, bf16[36,3072]{1,0:T(8,128)(2,1)S(1)}, u32[]{:S(2)}, u32[]{:S(2)}) collective-permute-start(bf16[36,3072]{1,0:T(8,128)(2,1)S(1)} %get-tuple-element.143), channel_id=1, source_target_pairs={{0,16},{2,18},{4,20},{6,22},{8,24},{10,26},{12,28},{14,30},{16,0},... | collective-permute-start | bytes 663560 | tf_op jit(solution)/shard_map/ppermute | solution.py:178
  368.1 9.0 %collective-permute-start.38 = (bf16[36,3072]{1,0:T(8,128)(2,1)S(1)}, bf16[36,3072]{1,0:T(8,128)(2,1)S(1)}, u32[]{:S(2)}, u32[]{:S(2)}) collective-permute-start(bf16[36,3072]{1,0:T(8,128)(2,1)S(1)} %get-tuple-element.142), channel_id=1, source_target_pairs={{0,24},{2,26},{4,28},{6,30},{8,16},{10,18},{12,20},{14,22},{16,8},... | collective-permute-start | bytes 663560 | tf_op jit(solution)/shard_map/ppermute | solution.py:178
  370.5 9.3 %collective-permute-start.35 = (bf16[36,576]{1,0:T(8,128)(2,1)S(1)}, bf16[36,576]{1,0:T(8,128)(2,1)S(1)}, u32[]{:S(2)}, u32[]{:S(2)}) collective-permute-start(bf16[36,576]{1,0:T(8,128)(2,1)S(1)} %fusion.40), channel_id=1, source_target_pairs={{0,1},{1,0},{2,3},{3,2},{4,5},{5,4},{6,7},{7,6},{8,9},{9,8},{10,11... | collective-permute-start | bytes 124424 | tf_op jit(solution)/shard_map/ppermute | solution.py:178
  372.5 8.1 %collective-permute-start.26 = (bf16[4,36,960]{2,1,0:T(8,128)(2,1)S(1)}, bf16[4,36,960]{2,1,0:T(8,128)(2,1)S(1)}, u32[]{:S(2)}, u32[]{:S(2)}) collective-permute-start(bf16[4,36,960]{2,1,0:T(8,128)(2,1)S(1)} %dynamic-slice_bitcast_fusion.5), channel_id=1, source_target_pairs={{0,4},{2,6},{4,0},{6,2},{8,12},{10,14},{12,8},{14,10},{16,20},{18,... | collective-permute-start | bytes 829448 | tf_op jit(solution)/shard_map/ppermute | solution.py:178
  378.2 9.6 %collective-permute-start.39 = (bf16[36,3072]{1,0:T(8,128)(2,1)S(1)}, bf16[36,3072]{1,0:T(8,128)(2,1)S(1)}, u32[]{:S(2)}, u32[]{:S(2)}) collective-permute-start(bf16[36,3072]{1,0:T(8,128)(2,1)S(1)} %fusion.30), channel_id=1, source_target_pairs={{0,1},{1,0},{2,3},{3,2},{4,5},{5,4},{6,7},{7,6},{8,9},{9,8},{10,11... | collective-permute-start | bytes 663560 | tf_op jit(solution)/shard_map/ppermute | solution.py:178
  380.7 7.8 %collective-permute-start.27 = (bf16[36,960]{1,0:T(8,128)(2,1)S(1)}, bf16[36,960]{1,0:T(8,128)(2,1)S(1)}, u32[]{:S(2)}, u32[]{:S(2)}) collective-permute-start(bf16[36,960]{1,0:T(8,128)(2,1)S(1)} %get-tuple-element.165), channel_id=1, source_target_pairs={{0,8},{2,10},{4,12},{6,14},{8,0},{10,2},{12,4},{14,6},{16,24},{18,... | collective-permute-start | bytes 207368 | tf_op jit(solution)/shard_map/ppermute | solution.py:178
  385.3 8.0 %collective-permute-start.28 = (bf16[36,960]{1,0:T(8,128)(2,1)S(1)}, bf16[36,960]{1,0:T(8,128)(2,1)S(1)}, u32[]{:S(2)}, u32[]{:S(2)}) collective-permute-start(bf16[36,960]{1,0:T(8,128)(2,1)S(1)} %get-tuple-element.167), channel_id=1, source_target_pairs={{0,16},{2,18},{4,20},{6,22},{8,24},{10,26},{12,28},{14,30},{16,0},... | collective-permute-start | bytes 207368 | tf_op jit(solution)/shard_map/ppermute | solution.py:178
  386.3 7.0 %collective-permute-start.29 = (bf16[36,960]{1,0:T(8,128)(2,1)S(1)}, bf16[36,960]{1,0:T(8,128)(2,1)S(1)}, u32[]{:S(2)}, u32[]{:S(2)}) collective-permute-start(bf16[36,960]{1,0:T(8,128)(2,1)S(1)} %get-tuple-element.166), channel_id=1, source_target_pairs={{0,24},{2,26},{4,28},{6,30},{8,16},{10,18},{12,20},{14,22},{16,8},... | collective-permute-start | bytes 207368 | tf_op jit(solution)/shard_map/ppermute | solution.py:178
  393.4 4.5 %collective-permute-start.30 = (bf16[36,960]{1,0:T(8,128)(2,1)S(1)}, bf16[36,960]{1,0:T(8,128)(2,1)S(1)}, u32[]{:S(2)}, u32[]{:S(2)}) collective-permute-start(bf16[36,960]{1,0:T(8,128)(2,1)S(1)} %fusion.37), channel_id=1, source_target_pairs={{0,1},{1,0},{2,3},{3,2},{4,5},{5,4},{6,7},{7,6},{8,9},{9,8},{10,11... | collective-permute-start | bytes 207368 | tf_op jit(solution)/shard_map/ppermute | solution.py:178
  (37 other events, 147.6 us)
